TPU v7x, 128 devices: a whole 4x4x4 slice. The times are simulated.
128 devices in a mesh: tm: 64 (over x, y, z), space: 2 (over core).
Axes of the slice: x: 4, y: 4, z: 4, core: 2. Of those that a mesh axis runs over, the one named last changes fastest.
Arguments:
- clean: bfloat16 [320, 16, 16, 1280], P('tm', 'space'), may hold values from -6 to 6
- noise: bfloat16 [320, 16, 16, 1280], P('tm', 'space'), may hold values from -6 to 6
- timestep: int32 [1], replicated, may hold values from 0 to 999
- spatial_weight: bfloat16 [1280, 3, 3, 640], replicated, may hold values from -0.0546875 to 0.0546875
- temporal_weight: bfloat16 [640, 3, 640], replicated, may hold values from -0.125 to 0.125
Outputs:
- loss: float32 [], replicated
- spatial_grad: float32 [1280, 3, 3, 640], P(('tm', 'space'))
- temporal_grad: float32 [640, 3, 640], P(('tm', 'space'))
All inputs are finite; a program needn't handle non-finite values.
Results may differ from a plain program's by a relative error of at most 0.0036.
Values may be sent and summed in bfloat16 or wider, within the bound.
No kernel may reach another device: no remote copies, remote signals or barrier semaphores. Data moves between devices by JAX's collectives and lax.ppermute only.
A program may use at most 256 MiB of HBM per device.

v0:
```python
import math

import jax
import jax.numpy as jnp
from jax import lax
from jax.sharding import PartitionSpec as P

CLIP = 80
STEPS = 1000


def with_halo(x, sides, width):
    for axis, dim in sides:
        size, length = (lax.axis_size(axis), x.shape[dim])
        up = [(i, (i + 1) % size) for i in range(size - 1)]
        down = [(j, i) for i, j in up]
        last = lax.slice_in_dim(x, length - width, length, axis=dim)
        first = lax.slice_in_dim(x, 0, width, axis=dim)
        before = lax.ppermute(last, axis, up)
        after = lax.ppermute(first, axis, down)
        x = jnp.concatenate([before, x, after], axis=dim)
    return x


def spatial_forward(padded, weight, rows, cols):
    total = jnp.zeros((padded.shape[0] * rows * cols, weight.shape[3]), jnp.float32)
    for first in range(3):
        for second in range(3):
            piece = padded[:, first : first + rows, second : second + cols, :].reshape(
                -1, padded.shape[3]
            )
            total = total + jnp.dot(
                piece, weight[:, first, second, :], preferred_element_type=jnp.float32
            )
    return total


def spatial_backward(padded, flat_grad, rows, cols):
    blocks = []
    for first in range(3):
        for second in range(3):
            piece = padded[:, first : first + rows, second : second + cols, :].reshape(
                -1, padded.shape[3]
            )
            blocks.append(
                lax.dot_general(
                    piece, flat_grad, (((0,), (0,)), ((), ())), preferred_element_type=jnp.float32
                )
            )
    return jnp.stack(blocks, axis=1).reshape(padded.shape[3], 3, 3, flat_grad.shape[1])


def outer_sum(left, right):
    return lax.dot_general(
        left, right, (((0,), (0,)), ((), ())), preferred_element_type=jnp.float32
    )


def trim_rims(padded, starts, ends):
    lowest = jnp.where(starts, jnp.zeros_like(padded[:1]), padded[:1])
    highest = jnp.where(ends, jnp.zeros_like(padded[-1:]), padded[-1:])
    return jnp.concatenate([lowest, padded[1:-1], highest], axis=0)


def on_device(clean, noise, timestep, spatial_weight, temporal_weight):
    frames_here, rows, cols, channels = clean.shape
    features = temporal_weight.shape[0]
    begin = lax.axis_index("tm") * frames_here
    starts = (begin + CLIP // 4) % CLIP == 0
    ends = (begin + frames_here + CLIP // 4) % CLIP == 0
    step_value = timestep[0].astype(jnp.float32)
    angle = math.pi / 2.0 * (step_value + 1.0) / (STEPS + 1.0)
    signal = jnp.cos(angle)
    sigma = jnp.sin(angle)
    clean32 = clean.astype(jnp.float32)
    noise32 = noise.astype(jnp.float32)
    noisy = (signal * clean32 + sigma * noise32).astype(jnp.bfloat16)
    row_padded = with_halo(noisy, (("space", 1),), 1)
    padded = jnp.pad(row_padded, ((0, 0), (0, 0), (1, 1), (0, 0)))
    hidden = spatial_forward(padded, spatial_weight, rows, cols)
    act = jax.nn.silu(hidden).astype(jnp.bfloat16).reshape(frames_here, rows * cols, features)
    pred = jnp.zeros((frames_here, rows * cols, features), jnp.float32)
    pad_act = trim_rims(with_halo(act, (("tm", 0),), 1), starts, ends)
    for tap in range(3):
        term = jnp.dot(
            pad_act[tap : tap + frames_here].reshape(-1, features),
            temporal_weight[:, tap, :],
            preferred_element_type=jnp.float32,
        )
        pred = pred + term.reshape(frames_here, rows * cols, features)
    target = (signal * noise32 - sigma * clean32)[..., :features].reshape(
        frames_here, rows * cols, features
    )
    diff = pred - target
    positions = frames_here * lax.axis_size("tm") * rows * lax.axis_size("space") * cols
    loss = lax.psum(jnp.sum(diff * diff), ("tm", "space")) / (positions * features)
    grad_pred = (2.0 * diff / math.sqrt(positions)).astype(jnp.bfloat16)
    flat_grad = grad_pred.reshape(-1, features)
    pad_grad = trim_rims(with_halo(grad_pred, (("tm", 0),), 1), starts, ends)
    grad_act = jnp.zeros((frames_here * rows * cols, features), jnp.float32)
    temporal_blocks = []
    for tap in range(3):
        shifted = pad_act[tap : tap + frames_here].reshape(-1, features)
        temporal_blocks.append(outer_sum(shifted, flat_grad))
        later = pad_grad[2 - tap : 2 - tap + frames_here].reshape(-1, features)
        grad_act = grad_act + lax.dot_general(
            later,
            temporal_weight[:, tap, :],
            (((1,), (1,)), ((), ())),
            preferred_element_type=jnp.float32,
        )
    temporal_local = jnp.stack(temporal_blocks, axis=1)
    sig = jax.nn.sigmoid(hidden)
    grad_hidden = (grad_act * sig * (1.0 + hidden * (1.0 - sig))).astype(jnp.bfloat16)
    spatial_local = spatial_backward(padded, grad_hidden, rows, cols)
    spatial_grad, temporal_grad = (
        lax.psum_scatter(spatial_local, ("tm", "space"), scatter_dimension=0, tiled=True),
        lax.psum_scatter(temporal_local, ("tm", "space"), scatter_dimension=0, tiled=True),
    )
    return (loss, spatial_grad, temporal_grad)


def solution(mesh):
    placed = (P("tm", "space", None, None), P("tm", "space", None, None), P(), P(), P())
    return jax.shard_map(
        on_device,
        mesh=mesh,
        in_specs=placed,
        out_specs=(P(), P(("tm", "space"), None, None, None), P(("tm", "space"), None, None)),
        check_vma=False,
    )
```

profile of v0, /device:TPU:0, one launch (start us, length us, event | category | flops | bytes accessed | tf_op | source)
XLA Modules:
  0.0 495.8 jit_solution(4579672109347895222)
XLA Ops:
  17.7 3.0 fusion.24
  21.7 4.1 fusion.18
  27.5 3.1 fusion.66
  30.6 4.1 fusion.20
  34.6 2.9 fusion.22
  40.4 2.9 fusion.28
  43.3 2.9 fusion.32
  49.1 4.8 multiply_convert_fusion.2
  55.2 5.4 %collective-permute-start.2 = (bf16[1,128,640]{2,1,0:T(8,128)(2,1)S(1)}, bf16[1,128,640]{2,1,0:T(8,128)(2,1)S(1)}, u32[]{:S(2)}, u32[]{:S(2)}) collective-permute-start(bf16[1,128,640]{2,1,0:T(8,128)(2,1)S(1)} %get-tuple-element.27), channel_id=1, source_target_pairs={{0,2},{2,4},{4,6},{6,8},{8,10},{10,12},{12,14},{14,16},{16,18},{18... | collective-permute-start | bytes 491528 | tf_op jit(solution)/shard_map/ppermute | solution.py:19
  61.5 3.1 collective-permute-done.2
  69.7 5.1 %collective-permute-start.5 = (bf16[1,128,640]{2,1,0:T(8,128)(2,1)}, bf16[1,128,640]{2,1,0:T(8,128)(2,1)}, u32[]{:S(2)}, u32[]{:S(2)}) collective-permute-start(bf16[1,128,640]{2,1,0:T(8,128)(2,1)} %get-tuple-element.24), channel_id=1, source_target_pairs={{0,2},{2,4},{4,6},{6,8},{8,10},{10,12},{12,14},{14,16},{16,18},{18... | collective-permute-start | bytes 491528 | tf_op jit(solution)/shard_map/ppermute | solution.py:19
  77.3 6.2 %copy.15 = f32[640,3,640]{2,1,0:T(4,128)} copy(f32[640,3,640]{2,0,1:T(8,128)S(1)} %pad_maximum_fusion) | data formatting | bytes 9830400 | tf_op jit(solution)/shard_map/stack | solution.py:112
  89.3 3.4 fusion.12
  92.7 3.3 fusion.11
  96.1 3.5 fusion.10
  99.6 3.3 fusion.9
  103.0 3.4 fusion.8
  106.3 3.4 fusion.7
  109.8 3.3 fusion.6
  113.1 3.4 fusion.5
  116.5 3.4 fusion.4
  119.9 38.9 %copy.12 = f32[1280,3,3,640]{3,2,1,0:T(4,128)} copy(f32[1280,3,3,640]{3,0,2,1:T(8,128)} %bitcast.42) | data formatting | bytes 58982400 | tf_op jit(solution)/shard_map/reshape | solution.py:50
  158.8 80.8 %psum.7 = f32[]{:T(128)} all-reduce(f32[]{:T(128)} %get-tuple-element.17), channel_id=1, replica_groups=mesh['tm'=64,'space'=2] {'tm','space'}, use_global_device_ids=true, to_apply=%region_1.2 | all-reduce | flops 1 | bytes 8 | tf_op jit(solution)/shard_map/psum | solution.py:96
  240.3 244.1 %all-reduce.6.cloned.1.call-done = (f32[1280,3,3,640]{3,2,1,0:T(4,128)}, f32[640,3,640]{2,1,0:T(4,128)}) async-done(((f32[1280,3,3,640]{3,2,1,0:T(4,128)}, f32[640,3,640]{2,1,0:T(4,128)}), (f32[1280,3,3,640]{3,2,1,0:T(4,128)}, f32[640,3,640]{2,1,0:T(4,128)})) %all-reduce.6.cloned.1.call-update) | async-done | bytes 34406416
  (67 shorter events, 36.8 us)
Async XLA Ops:
  7.2 477.2 %all-reduce.6.cloned.1.call-start = ((), (), s32[]{:S(2)}) async-start(), calls=%async_computation | async-start | bytes 91750400
  8.0 5.4 %copy-start.2 = (bf16[5,8,16,1280]{3,2,1,0:T(8,128)(2,1)S(1)}, bf16[5,8,16,1280]{3,2,1,0:T(8,128)(2,1)}, u32[]{:S(2)}) copy-start(bf16[5,8,16,1280]{3,2,1,0:T(8,128)(2,1)} %param.5) | copy-start | bytes 4915204
  10.7 10.7 %collective-permute-start = (bf16[5,1,16,1280]{3,2,1,0:T(8,128)(2,1)S(1)}, bf16[5,1,16,1280]{3,2,1,0:T(8,128)(2,1)S(1)}, u32[]{:S(2)}, u32[]{:S(2)}) collective-permute-start(bf16[5,1,16,1280]{3,2,1,0:T(8,128)(2,1)S(1)} %get-tuple-element.20), channel_id=1, source_target_pairs={{0,1},{2,3},{4,5},{6,7},{8,9},{10,11},{12,13},{14,15},{16,17},{18,... | collective-permute-start | bytes 614408 | tf_op jit(solution)/shard_map/ppermute | solution.py:19
  12.0 3.6 copy-start.3
  12.0 9.4 %collective-permute-start.1 = (bf16[5,1,16,1280]{3,2,1,0:T(8,128)(2,1)S(1)}, bf16[5,1,16,1280]{3,2,1,0:T(8,128)(2,1)S(1)}, u32[]{:S(2)}, u32[]{:S(2)}) collective-permute-start(bf16[5,1,16,1280]{3,2,1,0:T(8,128)(2,1)S(1)} %get-tuple-element.21), channel_id=1, source_target_pairs={{1,0},{3,2},{5,4},{7,6},{9,8},{11,10},{13,12},{15,14},{17,16},{19,... | collective-permute-start | bytes 614408 | tf_op jit(solution)/shard_map/ppermute | solution.py:20
  17.7 3.0 copy-start
  17.7 3.4 copy-start.1
  21.7 4.1 copy-start.10
  21.7 24.5 %copy-start.12 = (bf16[5,8,16,1280]{3,2,1,0:T(8,128)(2,1)}, bf16[5,8,16,1280]{3,2,1,0:T(8,128)(2,1)S(1)}, u32[]{:S(2)}) copy-start(bf16[5,8,16,1280]{3,2,1,0:T(8,128)(2,1)S(1)} %get-tuple-element.18) | copy-start | bytes 4915204
  30.5 9.9 %copy-start.5 = (bf16[5,8,16,1280]{3,2,1,0:T(8,128)(2,1)}, bf16[5,8,16,1280]{3,2,1,0:T(8,128)(2,1)S(1)}, u32[]{:S(2)}) copy-start(bf16[5,8,16,1280]{3,2,1,0:T(8,128)(2,1)S(1)} %get-tuple-element.14) | copy-start | bytes 4915204
  30.6 12.8 %copy-start.7 = (bf16[5,8,16,1280]{3,2,1,0:T(8,128)(2,1)}, bf16[5,8,16,1280]{3,2,1,0:T(8,128)(2,1)S(1)}, u32[]{:S(2)}) copy-start(bf16[5,8,16,1280]{3,2,1,0:T(8,128)(2,1)S(1)} %get-tuple-element.10) | copy-start | bytes 4915204
  49.1 11.5 %copy-start.4 = (bf16[640,3,640]{2,0,1:T(8,128)(2,1)S(1)}, bf16[640,3,640]{2,0,1:T(8,128)(2,1)}, u32[]{:S(2)}) copy-start(bf16[640,3,640]{2,0,1:T(8,128)(2,1)} %param.9) | copy-start | bytes 7372804
  53.9 11.6 %collective-permute-start.3 = (bf16[1,128,640]{2,1,0:T(8,128)(2,1)S(1)}, bf16[1,128,640]{2,1,0:T(8,128)(2,1)S(1)}, u32[]{:S(2)}, u32[]{:S(2)}) collective-permute-start(bf16[1,128,640]{2,1,0:T(8,128)(2,1)S(1)} %get-tuple-element.26), channel_id=1, source_target_pairs={{2,0},{4,2},{6,4},{8,6},{10,8},{12,10},{14,12},{16,14},{18,16},{20... | collective-permute-start | bytes 491528 | tf_op jit(solution)/shard_map/ppermute | solution.py:20
  55.2 9.4 %collective-permute-start.2 = (bf16[1,128,640]{2,1,0:T(8,128)(2,1)S(1)}, bf16[1,128,640]{2,1,0:T(8,128)(2,1)S(1)}, u32[]{:S(2)}, u32[]{:S(2)}) collective-permute-start(bf16[1,128,640]{2,1,0:T(8,128)(2,1)S(1)} %get-tuple-element.27), channel_id=1, source_target_pairs={{0,2},{2,4},{4,6},{6,8},{8,10},{10,12},{12,14},{14,16},{16,18},{18... | collective-permute-start | bytes 491528 | tf_op jit(solution)/shard_map/ppermute | solution.py:19
  69.7 14.7 %collective-permute-start.5 = (bf16[1,128,640]{2,1,0:T(8,128)(2,1)}, bf16[1,128,640]{2,1,0:T(8,128)(2,1)}, u32[]{:S(2)}, u32[]{:S(2)}) collective-permute-start(bf16[1,128,640]{2,1,0:T(8,128)(2,1)} %get-tuple-element.24), channel_id=1, source_target_pairs={{0,2},{2,4},{4,6},{6,8},{8,10},{10,12},{12,14},{14,16},{16,18},{18... | collective-permute-start | bytes 491528 | tf_op jit(solution)/shard_map/ppermute | solution.py:19
  74.8 10.6 %collective-permute-start.4 = (bf16[1,128,640]{2,1,0:T(8,128)(2,1)S(1)}, bf16[1,128,640]{2,1,0:T(8,128)(2,1)}, u32[]{:S(2)}, u32[]{:S(2)}) collective-permute-start(bf16[1,128,640]{2,1,0:T(8,128)(2,1)S(1)} %get-tuple-element.25), channel_id=1, source_target_pairs={{2,0},{4,2},{6,4},{8,6},{10,8},{12,10},{14,12},{16,14},{18,16},{20... | collective-permute-start | bytes 491528 | tf_op jit(solution)/shard_map/ppermute | solution.py:20
  86.5 1.4 copy-start.9
  87.9 1.4 copy-start.8
  89.3 3.4 copy-start.13
  92.7 3.3 copy-start.6
  109.8 3.3 copy-start.11
Sparse Core Ops, SparseCore 0:
  158.9 325.4 all-reduce.5
where the time goes:
time: 501 us; the launch traced here: 496 us
  waiting for transfers between devices  247 us (49%)
  blocking collectives  80.8 us (16%)
  matrix products  69.9 us (14%)
  local copies, waits for them, and re-layouts  53.3 us (11%)
  between operations  17.2 us (3%)
  starting transfers between devices  15.8 us (3%)
  other arithmetic  11.5 us (2%)
    unnamed x2, waiting for transfers between devices  244 us
    psum x1, blocking collectives, on_device(): lax.psum(jnp.sum(diff * diff), ('tm', 'space')) / (positions * features)  80.8 us
    reshape x1, local copies, waits for them, and re-layouts, spatial_backward(): jnp.stack(blocks, axis=1).reshape(padded.shape[3], 3, 3, flat_grad.shape[1])  38.9 us
    dot_general x9, matrix products, spatial_backward(): lax.dot_general(piece, flat_grad, (((0,), (0,)), ((), ())), preferred_ele...  30.5 us
    dot_general x9, matrix products, spatial_forward(): jnp.dot(piece, weight[:, first, second, :], preferred_element_type=jnp.fl...  30.4 us
    ppermute x3, starting transfers between devices, with_halo(): before = lax.ppermute(last, axis, up)  11.8 us
  transfers between devices with their start and end apart: 7, of which 2 were waited for; matrix products, arithmetic and copies ran while one was open for 4% of the time, Pallas kernels for 0%

commit v1 on v0

v1 whole, which is shorter than its diff:
```python
import functools
import math

import jax
import jax.numpy as jnp
import numpy as np
from jax import lax
from jax.experimental import pallas as pl
from jax.experimental.pallas import tpu as pltpu
from jax.sharding import PartitionSpec as P

CLIP = 80
STEPS = 1000
BF = jnp.bfloat16
F32 = jnp.float32
MIB = 1 << 20
STRIDES = (16, 4, 1)
RING = 4
ORDERS = ((0, 1, 2), (1, 2, 0), (2, 0, 1))
LOSS = 16
EXTRA = 64


def params(mib):
    return pltpu.CompilerParams(vmem_limit_bytes=mib * MIB)


def cost(flops, nbytes):
    return pl.CostEstimate(flops=int(flops), bytes_accessed=int(nbytes), transcendentals=0)


def spatial_forward_kernel(x_ref, above_ref, below_ref, w_ref, act_ref, der_ref, xp, acc):
    step = pl.program_id(0)
    group = step // 3
    first = jnp.where(group == 0, 1, jnp.where(group == 1, 0, 2))
    second = step % 3
    frames, span, channels = x_ref.shape
    cols = above_ref.shape[1]
    features = w_ref.shape[3]

    @pl.when(step == 0)
    def _():
        xp[:, 0:cols, :] = above_ref[...]
        xp[:, cols : cols + span, :] = x_ref[...]
        xp[:, cols + span : span + 2 * cols, :] = below_ref[...]

    start = pl.multiple_of(first * cols, cols)
    piece = xp[:, pl.ds(start, span), :].reshape(frames * span, channels)
    prod = jnp.dot(piece, w_ref[0, 0], preferred_element_type=F32)

    @pl.when(step < 3)
    def _():
        acc[second] = prod

    @pl.when(step >= 3)
    def _():
        acc[second] += prod

    @pl.when(step == 8)
    def _():
        col = lax.broadcasted_iota(jnp.int32, (span, features), 0) % cols

        def one(f, carry):
            rows = pl.ds(pl.multiple_of(f * span, span), span)
            left = jnp.where(col == 0, 0.0, pltpu.roll(acc[0, rows, :], 1, 0))
            right = jnp.where(col == cols - 1, 0.0, pltpu.roll(acc[2, rows, :], span - 1, 0))
            hidden = left + acc[1, rows, :] + right
            sig = 1.0 / (1.0 + jnp.exp(-hidden))
            act_ref[f] = (hidden * sig).astype(BF)
            der_ref[f] = sig * (1.0 + hidden * (1.0 - sig))
            return carry

        lax.fori_loop(0, frames, one, 0)


def spatial_forward(x, above, below, weight):
    frames, span, channels = x.shape
    cols = above.shape[1]
    features = weight.shape[3]
    whole = lambda s: (0, 0, 0)

    def tap(s):
        g = s // 3
        return (jnp.where(g == 0, 1, jnp.where(g == 1, 0, 2)), s % 3, 0, 0)

    return pl.pallas_call(
        spatial_forward_kernel,
        grid=(9,),
        in_specs=[
            pl.BlockSpec(x.shape, whole),
            pl.BlockSpec(above.shape, whole),
            pl.BlockSpec(below.shape, whole),
            pl.BlockSpec((1, 1, channels, features), tap),
        ],
        out_specs=[
            pl.BlockSpec((frames, span, features), whole),
            pl.BlockSpec((frames, span, features), whole),
        ],
        out_shape=[
            jax.ShapeDtypeStruct((frames, span, features), BF),
            jax.ShapeDtypeStruct((frames, span, features), F32),
        ],
        scratch_shapes=[
            pltpu.VMEM((frames, span + 2 * cols, channels), BF),
            pltpu.VMEM((3, frames * span, features), F32),
        ],
        compiler_params=params(24),
        cost_estimate=cost(
            2 * 9 * frames * span * channels * features, 2 * 9 * channels * features
        ),
        name="spatial_forward",
    )(x, above, below, weight)


def temporal_forward_kernel(
    scale, act_ref, before_ref, after_ref, w_ref, clean_ref, noise_ref, gp_ref, loss_ref, ap
):
    frames, span, features = act_ref.shape
    factor = scale[2]
    ap[0:1] = before_ref[...]
    ap[1 : frames + 1] = act_ref[...]
    ap[frames + 1 : frames + 2] = after_ref[...]
    pred = jnp.zeros((frames * span, features), F32)
    for tap in range(3):
        pred = pred + jnp.dot(
            ap[tap : tap + frames].reshape(frames * span, features),
            w_ref[tap],
            preferred_element_type=F32,
        )
    clean = clean_ref[...].reshape(frames * span, features).astype(F32)
    noise = noise_ref[...].reshape(frames * span, features).astype(F32)
    diff = pred - (scale[0] * noise - scale[1] * clean)
    gp_ref[...] = (2.0 * diff / factor).astype(BF).reshape(frames, span, features)
    loss_ref[...] = jnp.sum(diff * diff, axis=0, keepdims=True)


def temporal_forward(scale, act, before, after, weight, clean, noise):
    frames, span, features = act.shape
    whole = lambda i: (0, 0, 0)
    head = pl.BlockSpec((frames, span, features), whole)
    halo = pl.BlockSpec((1, span, features), whole)
    return pl.pallas_call(
        temporal_forward_kernel,
        grid=(1,),
        in_specs=[
            pl.BlockSpec(memory_space=pltpu.SMEM),
            head,
            halo,
            halo,
            pl.BlockSpec(weight.shape, whole),
            head,
            head,
        ],
        out_specs=[head, pl.BlockSpec((1, features), lambda i: (0, 0))],
        out_shape=[
            jax.ShapeDtypeStruct((frames, span, features), BF),
            jax.ShapeDtypeStruct((1, features), F32),
        ],
        scratch_shapes=[pltpu.VMEM((frames + 2, span, features), BF)],
        compiler_params=params(14),
        cost_estimate=cost(2 * 3 * frames * span * features * features, 6 * features * features),
        name="temporal_forward",
    )(scale, act, before, after, weight, clean, noise)


def thirds(value):
    high = value.astype(BF)
    rest = value - high.astype(F32)
    middle = rest.astype(BF)
    return high, middle, (rest - middle.astype(F32)).astype(BF)


def stacked(value, rows):
    high, middle, low = thirds(value)
    row = lax.broadcasted_iota(jnp.int32, (rows, value.shape[1]), 0)
    parts = [p.astype(F32) for p in (high, middle, low)]
    return jnp.where(
        row == 0, parts[0], jnp.where(row == 1, parts[1], jnp.where(row == 2, parts[2], 0.0))
    )


def joined(rows):
    return (rows[0:1] + rows[1:2]) + rows[2:3]


def select_act_kernel(
    core_ref, act_ref, before_ref, after_ref, choice_ref, loss_ref, own_ref, send_ref, ap
):
    core = core_ref[0]
    frames, span, features = act_ref.shape
    half = features // 2
    ap[0:1] = before_ref[...]
    ap[1 : frames + 1] = act_ref[...]
    ap[frames + 1 : frames + 2] = after_ref[...]
    act = ap[...].reshape(-1, features)
    for out, which in ((send_ref, 1 - core), (own_ref, core)):
        out[0:half, :] = lax.dot_general(
            choice_ref[which], act, (((1,), (1,)), ((), ())), preferred_element_type=F32
        ).astype(BF)
    send_ref[half:, :] = jnp.zeros((send_ref.shape[0] - half, send_ref.shape[1]), BF)
    send_ref[half : half + LOSS, 0:features] = stacked(loss_ref[...], LOSS).astype(BF)


def selected_act(core, act, before, after, choice, loss):
    frames, span, features = act.shape
    width = (frames + 2) * span
    vmem = pl.BlockSpec(memory_space=pltpu.VMEM)
    return pl.pallas_call(
        select_act_kernel,
        in_specs=[pl.BlockSpec(memory_space=pltpu.SMEM)] + [vmem] * 5,
        out_specs=[vmem, vmem],
        out_shape=[
            jax.ShapeDtypeStruct((features // 2, width), BF),
            jax.ShapeDtypeStruct((features // 2 + LOSS, width), BF),
        ],
        scratch_shapes=[pltpu.VMEM((frames + 2, span, features), BF)],
        compiler_params=params(16),
        cost_estimate=cost(2 * features * features * width, 4 * features * width),
        name="select_act",
    )(core, act, before, after, choice, loss)


def temporal_grad_kernel(
    bits_ref,
    own_ref,
    other_ref,
    gp_ref,
    gp_other_ref,
    reorder_ref,
    loss_ref,
    send_ref,
    keep_ref,
    sum_ref,
    total,
):
    frames, span, features = gp_ref.shape
    half = own_ref.shape[0]
    rows = half // 2
    gp = gp_ref[...].reshape(frames * span, features)
    gp_other = gp_other_ref[...].reshape(frames * span, features)
    for tap in range(3):
        lanes = slice(tap * span, (tap + frames) * span)
        mine, theirs = own_ref[:, lanes], other_ref[0:half, lanes]
        if tap > 0:
            order = reorder_ref[bits_ref[3], tap - 1]
            mine = jnp.dot(order, mine, preferred_element_type=F32).astype(BF)
            theirs = jnp.dot(order, theirs, preferred_element_type=F32).astype(BF)
        total[...] = jnp.dot(mine, gp, preferred_element_type=F32) + jnp.dot(
            theirs, gp_other, preferred_element_type=F32
        )
        bit = bits_ref[tap]
        kept = pl.ds(pl.multiple_of(bit * rows, rows), rows)
        sent = pl.ds(pl.multiple_of((1 - bit) * rows, rows), rows)
        keep_ref[tap] = total[kept, :]
        send_ref[tap, 0:rows, :] = total[sent, :].astype(BF)
        send_ref[tap, rows:, :] = jnp.zeros((send_ref.shape[1] - rows, features), BF)
    met = other_ref[half : half + LOSS, 0:features].astype(F32)
    loss = loss_ref[...] + joined(met)
    sum_ref[...] = loss
    send_ref[0, rows : rows + LOSS, :] = stacked(loss, LOSS).astype(BF)


def temporal_grad_local(bits, own, other, gp, gp_other, reorder, loss):
    frames, span, features = gp.shape
    rows = features // 4
    return pl.pallas_call(
        temporal_grad_kernel,
        in_specs=[pl.BlockSpec(memory_space=pltpu.SMEM)]
        + [pl.BlockSpec(memory_space=pltpu.VMEM)] * 6,
        out_shape=[
            jax.ShapeDtypeStruct((3, 3 * EXTRA, features), BF),
            jax.ShapeDtypeStruct((3, rows, features), F32),
            jax.ShapeDtypeStruct((1, features), F32),
        ],
        out_specs=[pl.BlockSpec(memory_space=pltpu.VMEM)] * 3,
        scratch_shapes=[pltpu.VMEM((features // 2, features), F32)],
        compiler_params=params(14),
        cost_estimate=cost(
            2 * 3 * frames * span * features * features, 6 * features * features
        ),
        name="temporal_grad",
    )(bits, own, other, gp, gp_other, reorder, loss)


def temporal_backward_kernel(gp_ref, before_ref, after_ref, w_ref, der_ref, out_ref, pad):
    frames, span, features = gp_ref.shape
    pad[0:1] = before_ref[...]
    pad[1 : frames + 1] = gp_ref[...]
    pad[frames + 1 : frames + 2] = after_ref[...]
    total = jnp.zeros((frames * span, features), F32)
    for tap in range(3):
        total = total + lax.dot_general(
            pad[2 - tap : 2 - tap + frames].reshape(frames * span, features),
            w_ref[tap],
            (((1,), (1,)), ((), ())),
            preferred_element_type=F32,
        )
    der = der_ref[...].reshape(frames * span, features)
    out_ref[...] = (total * der).astype(BF).reshape(frames, span, features)


def temporal_backward(gp, before, after, weight, der):
    frames, span, features = gp.shape
    return pl.pallas_call(
        temporal_backward_kernel,
        out_shape=jax.ShapeDtypeStruct((frames, span, features), BF),
        scratch_shapes=[pltpu.VMEM((frames + 2, span, features), BF)],
        compiler_params=params(14),
        cost_estimate=cost(2 * 3 * frames * span * features * features, 6 * features * features),
        name="temporal_backward",
    )(gp, before, after, weight, der)


def select_latent_kernel(core_ref, x_ref, choice_ref, own_ref, send_ref):
    core = core_ref[0]
    x = x_ref[...].reshape(-1, x_ref.shape[2])
    for out, which in ((send_ref, 1 - core), (own_ref, core)):
        out[...] = lax.dot_general(
            choice_ref[which], x, (((1,), (1,)), ((), ())), preferred_element_type=F32
        ).astype(BF)


def selected_latent(core, x, choice):
    frames, span, channels = x.shape
    shape = jax.ShapeDtypeStruct((channels // 2, frames * span), BF)
    vmem = pl.BlockSpec(memory_space=pltpu.VMEM)
    return pl.pallas_call(
        select_latent_kernel,
        in_specs=[pl.BlockSpec(memory_space=pltpu.SMEM), vmem, vmem],
        out_specs=[vmem, vmem],
        out_shape=[shape, shape],
        compiler_params=params(20),
        cost_estimate=cost(2 * frames * span * channels * channels, 4 * channels * channels),
        name="select_latent",
    )(core, x, choice)


def arrange_latent_kernel(core_ref, own_ref, other_ref, reorder_ref, out_ref):
    core = core_ref[0]
    span = out_ref.shape[2] // 10
    for f in range(5):
        here = pl.multiple_of((2 * f + core) * span, span)
        there = pl.multiple_of((2 * f + 1 - core) * span, span)
        out_ref[0, :, pl.ds(here, span)] = own_ref[:, f * span : (f + 1) * span]
        out_ref[0, :, pl.ds(there, span)] = other_ref[:, f * span : (f + 1) * span]
    for third in range(1, 3):
        out_ref[third] = jnp.dot(
            reorder_ref[0, third - 1], out_ref[0], preferred_element_type=F32
        ).astype(BF)


def arranged_latent(core, own, other, reorder):
    half, positions = own.shape
    return pl.pallas_call(
        arrange_latent_kernel,
        grid_spec=pltpu.PrefetchScalarGridSpec(
            num_scalar_prefetch=1,
            grid=(1,),
            in_specs=[
                pl.BlockSpec(own.shape, lambda i, c: (0, 0)),
                pl.BlockSpec(own.shape, lambda i, c: (0, 0)),
                pl.BlockSpec((1, 2, half, half), lambda i, c: (c[0], 0, 0, 0)),
            ],
            out_specs=pl.BlockSpec((3, half, 2 * positions), lambda i, c: (0, 0, 0)),
        ),
        out_shape=jax.ShapeDtypeStruct((3, half, 2 * positions), BF),
        compiler_params=params(24),
        cost_estimate=cost(8 * half * half * positions, 20 * half * positions),
        name="arrange_latent",
    )(core, own, other, reorder)


def spatial_backward_kernel(has_extra, where, lat_ref, own_ref, other_ref, *rest):
    extra_ref = rest[0] if has_extra else None
    outs, pad = rest[-4:-1], rest[-1]
    step = pl.program_id(0)
    first = step // 3
    second = step % 3
    core = where[0]
    frames, span, features = own_ref.shape
    cols = (pad.shape[2] - 2 * span) // 2
    height = lat_ref.shape[1]

    @pl.when(step == 0)
    def _():
        col = lax.broadcasted_iota(jnp.int32, (span, features), 0) % cols
        rim = jnp.zeros((cols, features), BF)

        def one(f, carry):
            for b in range(3):
                pad[b, f, 0:cols, :] = rim
                pad[b, f, cols + 2 * span : 2 * cols + 2 * span, :] = rim
            for ref, place in ((own_ref, core), (other_ref, 1 - core)):
                rows = pl.ds(pl.multiple_of(cols + place * span, cols), span)
                here = ref[f]
                wide = here.astype(F32)
                later = jnp.where(col == cols - 1, 0.0, pltpu.roll(wide, span - 1, 0))
                sooner = jnp.where(col == 0, 0.0, pltpu.roll(wide, 1, 0))
                pad[0, f, rows, :] = later.astype(BF)
                pad[1, f, rows, :] = here
                pad[2, f, rows, :] = sooner.astype(BF)
            return carry

        lax.fori_loop(0, frames, one, 0)

    start = pl.multiple_of((2 - first) * cols, cols)
    grad = pad[second, :, pl.ds(start, 2 * span), :].reshape(2 * frames * span, features)
    total = jnp.dot(lat_ref[0], grad, preferred_element_type=F32)
    for row in range(3):

        @pl.when(first == row)
        def _():
            outs[row][0, 0:height, :] = total.astype(outs[row].dtype)
            if has_extra:
                outs[row][0, height:, :] = extra_ref[0]


def spatial_backward(where, lat, own, other, extra, kind, name):
    frames, span, features = own.shape
    rows = lat.shape[1] // 2
    cols = 16
    tall = rows + (0 if extra is None else EXTRA)

    def out_map(row):
        return lambda s, w: (jnp.clip(s - 3 * row, 0, 2), 0, 0)

    more_specs = [] if extra is None else [
        pl.BlockSpec((1, EXTRA, features), lambda s, w: (s // 3, s % 3, 0))
    ]
    more = [] if extra is None else [extra]
    return pl.pallas_call(
        functools.partial(spatial_backward_kernel, extra is not None),
        grid_spec=pltpu.PrefetchScalarGridSpec(
            num_scalar_prefetch=1,
            grid=(9,),
            in_specs=[
                pl.BlockSpec((1, rows, lat.shape[2]), lambda s, w: (s // 3, w[1 + s // 3], 0)),
                pl.BlockSpec(own.shape, lambda s, w: (0, 0, 0)),
                pl.BlockSpec(own.shape, lambda s, w: (0, 0, 0)),
            ]
            + more_specs,
            out_specs=[pl.BlockSpec((1, tall, features), out_map(r)) for r in range(3)],
            scratch_shapes=[pltpu.VMEM((3, frames, 2 * span + 2 * cols, features), BF)],
        ),
        out_shape=[jax.ShapeDtypeStruct((3, tall, features), kind) for _ in range(3)],
        compiler_params=params(24),
        cost_estimate=cost(
            2 * 9 * rows * 2 * frames * span * features,
            9 * rows * features * jnp.dtype(kind).itemsize,
        ),
        name=name,
    )(where, lat, own, other, *more)


def bit_of(value, kind):
    if kind == 0:
        return value // 2
    return (value + 1) // 2 % 2


def swap_pairs(axis, step, size):
    pairs = []
    stride = STRIDES[axis]
    for device in range(size):
        tm, core = divmod(device, 2)
        value = tm // stride % RING
        partner = (value ^ 1) if (step + core) % 2 == 0 else (RING - 1 - value)
        pairs.append((device, (tm + (partner - value) * stride) * 2 + core))
    return pairs


def owners(order, core):
    found = []
    for n in range(RING**3):
        place = 0
        for k, axis in enumerate(order):
            digit = n // RING ** (2 - k) % RING
            first, second = divmod(digit, 2)
            low, high = (second, first) if core == 0 else (first, second)
            value = 2 * low + (low ^ high)
            place += value * STRIDES[axis]
        found.append(2 * place + core)
    return np.array(found)


def one_hot(rows, width):
    return (rows[:, None] == np.arange(width)[None, :]).astype(np.float32)


def selections(channels):
    each = channels // (2 * RING**3)
    return np.stack(
        [
            one_hot((owners(ORDERS[0], c)[:, None] * each + np.arange(each)).reshape(-1), channels)
            for c in range(2)
        ]
    )


def reorders(channels):
    each = channels // (2 * RING**3)
    found = []
    for c in range(2):
        base = list(owners(ORDERS[0], c))
        for order in ORDERS[1:]:
            at = np.array([base.index(o) for o in owners(order, c)])
            rows = (at[:, None] * each + np.arange(each)).reshape(-1)
            found.append(one_hot(rows, channels // 2))
    return np.stack(found).reshape(2, 2, channels // 2, channels // 2)


def up_to(n, multiple):
    return -(-n // multiple) * multiple


def payload_rows(rows, more, has_loss):
    return 3 * up_to(rows, 16) + (LOSS if has_loss else 0) + up_to(more, 16)


def places(rows, has_loss, initial):
    if initial:
        tall = rows + EXTRA
        pieces = [(rows, EXTRA, 0), (tall + rows, EXTRA, EXTRA), (2 * tall + rows, 32, 2 * EXTRA)]
        return [0, tall, 2 * tall], 2 * tall + rows + 32, pieces
    slab = up_to(rows, 16)
    behind = 3 * slab + (LOSS if has_loss else 0)
    return [0, slab, 2 * slab], 3 * slab, [(behind, None, 0)]


def combine_kernel(rows, more, has_loss, initial, bit_ref, met_ref, sp_ref, tp_ref, *rest):
    if has_loss:
        loss_ref, send_ref, sp_out, tp_out, loss_out, full, full_more = rest
    else:
        send_ref, sp_out, tp_out, full, full_more = rest
    bit = bit_ref[0]
    slabs, loss_at, pieces = places(rows, has_loss, initial)

    def halve(ref, count, send_at, out_ref):
        part = count // 2
        sent = up_to(part, 16)
        kept = up_to(part, 8)
        if part % 16 == 0:
            mine = ref[pl.ds(pl.multiple_of(bit * part, part), part), :]
            theirs = ref[pl.ds(pl.multiple_of((1 - bit) * part, part), part), :]
        else:
            whole = ref[...]
            tall = whole.shape[0]
            mine = pltpu.roll(whole, (tall - bit * part) % tall, 0)[:kept]
            theirs = pltpu.roll(whole, (tall - (1 - bit) * part) % tall, 0)[:sent]
        send_ref[send_at : send_at + sent, :] = theirs.astype(send_ref.dtype)
        return mine

    next_slab = up_to(rows // 2, 16)
    for b in range(3):
        tall = full.shape[1]
        full[b] = sp_ref[b] + met_ref[slabs[b] : slabs[b] + tall, :].astype(F32)
        sp_out[b] = halve(full.at[b], rows, b * next_slab, sp_out)
    for at, count, to in pieces:
        count = full_more.shape[0] if count is None else count
        full_more[to : to + count, :] = tp_ref[to : to + count, :] + met_ref[
            at : at + count, :
        ].astype(F32)
    behind = 3 * next_slab
    if has_loss:
        loss = loss_ref[...] + joined(met_ref[loss_at : loss_at + LOSS, :].astype(F32))
        loss_out[...] = loss
        send_ref[behind : behind + LOSS, :] = stacked(loss, LOSS).astype(send_ref.dtype)
        behind += LOSS
    tp_out[...] = halve(full_more, more, behind, tp_out)


def combine(bit, met, sp, tp, loss, rows, more, initial, kind, name):
    has_loss = loss is not None
    width = met.shape[1]
    out_shape = [
        jax.ShapeDtypeStruct((payload_rows(rows // 2, more // 2, has_loss), width), kind),
        jax.ShapeDtypeStruct((3, up_to(rows // 2, 8), width), F32),
        jax.ShapeDtypeStruct((up_to(more // 2, 8), width), F32),
    ]
    operands = [bit, met, sp, tp]
    if has_loss:
        out_shape.append(jax.ShapeDtypeStruct((1, width), F32))
        operands.append(loss)
    vmem = pl.BlockSpec(memory_space=pltpu.VMEM)
    done = pl.pallas_call(
        functools.partial(combine_kernel, rows, more, has_loss, initial),
        in_specs=[pl.BlockSpec(memory_space=pltpu.SMEM)] + [vmem] * (len(operands) - 1),
        out_specs=[vmem] * len(out_shape),
        out_shape=out_shape,
        scratch_shapes=[pltpu.VMEM(sp.shape, F32), pltpu.VMEM(tp.shape, F32)],
        compiler_params=params(14),
        cost_estimate=cost(0, 8 * sp.size),
        name=name,
    )(*operands)
    return done if has_loss else (*done, None)


def on_device(clean, noise, timestep, spatial_weight, temporal_weight):
    frames, rows, cols, channels = clean.shape
    features = temporal_weight.shape[0]
    span = rows * cols
    blocks = lax.axis_size("tm")
    size = 2 * blocks
    tm = lax.axis_index("tm")
    core = lax.axis_index("space")
    both = ("tm", "space")
    step_value = timestep[0].astype(F32)
    angle = math.pi / 2.0 * (step_value + 1.0) / (STEPS + 1.0)
    signal = jnp.cos(angle)
    sigma = jnp.sin(angle)
    positions = frames * blocks * rows * 2 * cols
    scale = jnp.stack([signal, sigma, jnp.float32(math.sqrt(positions))])
    w_spatial = jnp.transpose(spatial_weight, (1, 2, 0, 3))
    w_temporal = jnp.transpose(temporal_weight, (1, 0, 2))

    def mix(c, n):
        return (signal * c.astype(F32) + sigma * n.astype(F32)).astype(BF)

    edge_at = (1 - core) * (rows - 1)
    edge = mix(
        lax.dynamic_slice_in_dim(clean, edge_at, 1, axis=1),
        lax.dynamic_slice_in_dim(noise, edge_at, 1, axis=1),
    )
    met = lax.ppermute(edge, "space", [(0, 1), (1, 0)]).reshape(frames, cols, channels)
    above = jnp.where(core == 0, jnp.zeros_like(met), met)
    below = jnp.where(core == 0, met, jnp.zeros_like(met))
    noisy = mix(clean, noise).reshape(frames, span, channels)
    cross = [(0, 1), (1, 0)]
    core_index = jnp.reshape(core, (1,)).astype(jnp.int32)
    act, der = spatial_forward(noisy, above, below, w_spatial)

    per_clip = CLIP // frames
    shift = CLIP // 4 // frames
    up = [(i, i + 1) for i in range(blocks - 1) if (i + 1 + shift) % per_clip != 0]
    down = [(j, i) for i, j in up]
    act_before = lax.ppermute(act[-1:], "tm", up)
    act_after = lax.ppermute(act[:1], "tm", down)
    lat_own, lat_send = selected_latent(core_index, noisy, jnp.asarray(selections(channels), BF))
    lat_other = lax.ppermute(lat_send, "space", cross)
    flat = (frames, span, channels)
    gp, loss_lanes = temporal_forward(
        scale, act, act_before, act_after, w_temporal, clean.reshape(flat), noise.reshape(flat)
    )
    gp_before = lax.ppermute(gp[-1:], "tm", up)
    gp_after = lax.ppermute(gp[:1], "tm", down)
    gp_other = lax.ppermute(gp, "space", cross)
    act_own, act_send = selected_act(
        core_index, act, act_before, act_after, jnp.asarray(selections(features), BF), loss_lanes
    )
    act_other = lax.ppermute(act_send, "space", cross)
    lat = arranged_latent(core_index, lat_own, lat_other, jnp.asarray(reorders(channels), BF))
    gh = temporal_backward(gp, gp_before, gp_after, w_temporal, der)
    gh_other = lax.ppermute(gh, "space", cross)

    bits = []
    for order in ORDERS:
        own = []
        for axis in order:
            value = tm // STRIDES[axis] % RING
            low, high = bit_of(value, 0), bit_of(value, 1)
            own.append(jnp.where(core == 0, high, low))
            own.append(jnp.where(core == 0, low, high))
        bits.append([b.astype(jnp.int32) for b in own])
    first_bits = jnp.stack([b[0] for b in bits])
    extra, extra_keep, loss = temporal_grad_local(
        jnp.concatenate([first_bits, core_index]),
        act_own,
        act_other,
        gp,
        gp_other,
        jnp.asarray(reorders(features), BF),
        loss_lanes,
    )
    sends = spatial_backward(
        jnp.concatenate([core_index, 1 - first_bits]), lat, gh, gh_other, extra, BF, "spatial_send"
    )
    keeps = spatial_backward(
        jnp.concatenate([core_index, first_bits]), lat, gh, gh_other, None, F32, "spatial_keep"
    )

    state = [
        (sends[t].reshape(-1, features), keeps[t], extra_keep[t], loss if t == 0 else None)
        for t in range(3)
    ]
    count, more = channels // 4, features // 4
    for step in range(6):
        met = [
            lax.ppermute(state[t][0], both, swap_pairs(ORDERS[t][step // 2], step, size))
            for t in range(3)
        ]
        if step == 5:
            break
        kind = BF if step < 4 else F32
        for t in range(3):
            _, sp, tp, total = state[t]
            bit = jnp.reshape(bits[t][step + 1], (1,))
            name = "combine_%d_%d" % (step, t)
            state[t] = combine(bit, met[t], sp, tp, total, count, more, step == 0, kind, name)
        count, more = count // 2, more // 2

    spatial_parts, temporal_parts = [], []
    for t in range(3):
        _, sp, tp, total = state[t]
        slabs, loss_at, ((behind, _, _),) = places(count, total is not None, False)
        spatial_parts.append(
            jnp.stack([sp[b, :count] + met[t][s : s + count] for b, s in enumerate(slabs)])
        )
        temporal_parts.append(tp[:more] + met[t][behind : behind + more])
        if total is not None:
            loss_sum = jnp.sum(total + joined(met[t][loss_at : loss_at + LOSS]))
    spatial_grad = jnp.transpose(jnp.stack(spatial_parts), (2, 0, 1, 3))
    temporal_grad = jnp.transpose(jnp.stack(temporal_parts), (1, 0, 2))
    return (loss_sum / (positions * features), spatial_grad, temporal_grad)


def solution(mesh):
    placed = (P("tm", "space", None, None), P("tm", "space", None, None), P(), P(), P())
    return jax.shard_map(
        on_device,
        mesh=mesh,
        in_specs=placed,
        out_specs=(P(), P(("tm", "space"), None, None, None), P(("tm", "space"), None, None)),
        check_vma=False,
    )
```

time: 501 us -> 190 us (0.38)
  waiting for transfers between devices: 247 us -> 34.2 us
  blocking collectives: 80.8 us -> 0 us
  Pallas kernels: 0 us -> 77.2 us
  matrix products: 69.9 us -> 0 us
  starting transfers between devices: 15.8 us -> 52.5 us
  local copies, waits for them, and re-layouts: 53.3 us -> 16.7 us
  between operations: 17.2 us -> 3.68 us
  other arithmetic: 11.5 us -> 4.79 us
    unnamed x2 -> x0, waiting for transfers between devices: 244 us -> none
    psum x1 -> x0, blocking collectives: 80.8 us -> none  [on_device(): lax.psum(jnp.sum(diff * diff), ('tm', 'space')) / (positions * features)]
    pallas_call x0 -> x24, Pallas kernels: none -> 77.2 us  [the longest x2 23.9 us: spatial_backward(): pl.pallas_call(functools.partial(spatial_backward_kernel, extra is not No...]
    dot_general x27 -> x0, matrix products: 69.9 us -> none  [the longest x9 30.5 us: spatial_backward(): lax.dot_general(piece, flat_grad, (((0,), (0,)), ((), ())), preferred_ele...]
    reshape x1 -> x0, local copies, waits for them, and re-layouts: 38.9 us -> none  [spatial_backward(): jnp.stack(blocks, axis=1).reshape(padded.shape[3], 3, 3, flat_grad.shape[1])]
    ppermute x6 -> x27, starting transfers between devices: 15.8 us -> 52.5 us  [the longest x18 39.4 us: on_device(): lax.ppermute(state[t][0], both, swap_pairs(ORDERS[t][step // 2], step, si...]
    ppermute x6 -> x27, waiting for transfers between devices: 3.1 us -> 34.2 us  [the longest x18 30.1 us: on_device(): lax.ppermute(state[t][0], both, swap_pairs(ORDERS[t][step // 2], step, si...]
    unnamed x30 -> x46, local copies, waits for them, and re-layouts: 4.46 us -> 15.6 us
  transfers between devices with their start and end apart: 7 -> 27, of which waited for: 2 -> 11; matrix products, arithmetic and copies ran while one was open for 4% -> 2% of each run, Pallas kernels for 0% -> 26%
where the time goes in v1:
time: 190 us; the launch traced here: 189 us
  Pallas kernels  77.2 us (41%)
  starting transfers between devices  52.5 us (28%)
  waiting for transfers between devices  34.2 us (18%)
  local copies, waits for them, and re-layouts  16.7 us (9%)
  other arithmetic  4.79 us (3%)
  between operations  3.68 us (2%)
    ppermute x18, starting transfers between devices, on_device(): lax.ppermute(state[t][0], both, swap_pairs(ORDERS[t][step // 2], step, si...  39.4 us
    ppermute x18, waiting for transfers between devices, on_device(): lax.ppermute(state[t][0], both, swap_pairs(ORDERS[t][step // 2], step, si...  30.1 us
    pallas_call x2, Pallas kernels, spatial_backward(): pl.pallas_call(functools.partial(spatial_backward_kernel, extra is not No...  23.9 us
    unnamed x46, local copies, waits for them, and re-layouts  15.6 us
    pallas_call x1, Pallas kernels, spatial_forward(): pl.pallas_call(spatial_forward_kernel, grid=(9,), in_specs=[pl.BlockSpec(...  15.6 us
    pallas_call x15, Pallas kernels, combine(): pl.pallas_call(functools.partial(combine_kernel, rows, more, has_loss, in...  13.4 us
    pallas_call x1, Pallas kernels, temporal_grad_local(): pl.pallas_call(temporal_grad_kernel, in_specs=[pl.BlockSpec(memory_space=...  6.65 us
    ppermute x1, starting transfers between devices, on_device(): gp_before = lax.ppermute(gp[-1:], 'tm', up)  5.03 us
  transfers between devices with their start and end apart: 27, of which 11 were waited for; matrix products, arithmetic and copies ran while one was open for 2% of the time, Pallas kernels for 26%

profile of v1, /device:TPU:0, one launch (start us, length us, event | category | flops | bytes accessed | tf_op | source)
XLA Modules:
  0.0 189.1 jit_solution(15683254319388921763)
XLA Ops:
  5.2 5.2 %copy-done.16 = bf16[1280,3,3,640]{3,0,2,1:T(8,128)(2,1)S(1)} copy-done((bf16[1280,3,3,640]{3,0,2,1:T(8,128)(2,1)S(1)}, bf16[1280,3,3,640]{3,0,2,1:T(8,128)(2,1)}, u32[]{:S(2)}) %copy-start.16) | copy-done | bytes 14745624
  10.4 15.6 %spatial_forward.1 = (bf16[5,128,640]{2,1,0:T(8,128)(2,1)S(1)}, f32[5,128,640]{2,1,0:T(8,128)S(1)}) custom-call(bf16[5,128,1280]{2,1,0:T(8,128)(2,1)S(1)} %bitcast.87, bf16[5,16,1280]{2,1,0:T(8,128)(2,1)S(1)} %get-tuple-element.157.above_ref, bf16[5,16,1280]{2,1,0:T(8,128)(2,1)S(1)} %get-tuple-element.156.below_ref, bf16[3,3,1280,640]{3,2,1,0:T(8,128)(2,1)S(1)} %bitcast.89), custom_call_target="tpu_custom_call" | custom-call | flops 9437184000 | bytes 14745600 | tf_op jit(solution)/shard_map/spatial_forward/pallas_call | solution.py:86
  27.3 4.6 %collective-permute-start.2 = (bf16[1,128,640]{2,1,0:T(8,128)(2,1)S(1)}, bf16[1,128,640]{2,1,0:T(8,128)(2,1)S(1)}, u32[]{:S(2)}, u32[]{:S(2)}) collective-permute-start(bf16[1,128,640]{2,1,0:T(8,128)(2,1)S(1)} %get-tuple-element.146), channel_id=1, source_target_pairs={{0,2},{2,4},{4,6},{6,8},{8,10},{10,12},{12,14},{14,16},{16,18},{18... | collective-permute-start | bytes 491528 | tf_op jit(solution)/shard_map/ppermute | solution.py:636
  31.9 2.8 %select_latent.1 = (bf16[640,640]{1,0:T(8,128)(2,1)S(1)}, bf16[640,640]{1,0:T(8,128)(2,1)}) custom-call(s32[1]{0:T(128)} %bitcast.5.core_ref, bf16[5,128,1280]{2,1,0:T(8,128)(2,1)S(1)} %bitcast.88, bf16[2,640,1280]{2,1,0:T(8,128)(2,1)S(1)} %copy-done.17), custom_call_target="tpu_custom_call" | custom-call | flops 2097152000 | bytes 6553600 | tf_op jit(solution)/shard_map/select_latent/pallas_call | solution.py:327
  36.0 3.9 %temporal_forward.1 = (bf16[5,128,640]{2,1,0:T(8,128)(2,1)}, f32[1,640]{1,0:T(1,128)S(1)}) custom-call(f32[3]{0:T(128)S(1)} %pad_maximum_fusion.scale, bf16[5,128,640]{2,1,0:T(8,128)(2,1)S(1)} %get-tuple-element.72.act_ref, bf16[1,128,640]{2,1,0:T(8,128)(2,1)S(1)} %collective-permute-done.2.before_ref, ...), custom_call_target="tpu_custom_call" | custom-call | flops 1572864000 | bytes 2457600 | tf_op jit(solution)/shard_map/temporal_forward/pallas_call | solution.py:142
  42.2 5.0 %collective-permute-start.4 = (bf16[1,128,640]{2,1,0:T(8,128)(2,1)S(1)}, bf16[1,128,640]{2,1,0:T(8,128)(2,1)S(1)}, u32[]{:S(2)}, u32[]{:S(2)}) collective-permute-start(bf16[1,128,640]{2,1,0:T(8,128)(2,1)S(1)} %get-tuple-element.144), channel_id=1, source_target_pairs={{0,2},{2,4},{4,6},{6,8},{8,10},{10,12},{12,14},{14,16},{16,18},{18... | collective-permute-start | bytes 491528 | tf_op jit(solution)/shard_map/ppermute | solution.py:644
  50.6 4.6 %temporal_backward.1.own_ref = bf16[5,128,640]{2,1,0:T(8,128)(2,1)} custom-call(bf16[5,128,640]{2,1,0:T(8,128)(2,1)} %get-tuple-element.73.gp_ref, bf16[1,128,640]{2,1,0:T(8,128)(2,1)S(1)} %collective-permute-done.4.before_ref, bf16[1,128,640]{2,1,0:T(8,128)(2,1)S(1)} %collective-permute-done.5.after_ref, bf16[3,640,640]{2,1,0:T(8,128)(2,1)S(1)} %bitcast.84, ...), custom_call_target="tpu_custom_call" | custom-call | flops 1572864000 | bytes 2457600 | tf_op jit(solution)/shard_map/temporal_backward/pallas_call | solution.py:304
  60.0 4.3 %arrange_latent.1.lat_ref = bf16[3,640,1280]{2,1,0:T(8,128)(2,1)S(1)} custom-call(s32[1]{0:T(128)} %bitcast.5.core_ref, bf16[640,640]{1,0:T(8,128)(2,1)S(1)} %copy-done.13, bf16[640,640]{1,0:T(8,128)(2,1)} %collective-permute-done.other_ref, bf16[2,2,640,640]{3,2,1,0:T(8,128)(2,1)S(1)} %copy-done.5), custom_call_target="tpu_custom_call" | custom-call | flops 2097152000 | bytes 8192000 | tf_op jit(solution)/shard_map/arrange_latent/pallas_call | solution.py:354
  64.3 6.6 %temporal_grad.1 = (bf16[3,192,640]{2,1,0:T(8,128)(2,1)S(1)}, f32[3,160,640]{2,1,0:T(8,128)S(1)}, f32[1,640]{1,0:T(1,128)S(1)}) custom-call(s32[4]{0:T(128)S(1)} %pad_add_fusion.1.bits_ref, bf16[320,896]{1,0:T(8,128)(2,1)S(1)} %copy-done.21, bf16[336,896]{1,0:T(8,128)(2,1)} %collective-permute-done.7.other_ref, ...), custom_call_target="tpu_custom_call" | custom-call | flops 1572864000 | bytes 2457600 | tf_op jit(solution)/shard_map/temporal_grad/pallas_call | solution.py:266
  71.0 12.8 %spatial_send.1 = (bf16[3,384,640]{2,1,0:T(8,128)(2,1)}, bf16[3,384,640]{2,1,0:T(8,128)(2,1)}, bf16[3,384,640]{2,1,0:T(8,128)(2,1)}) custom-call(s32[4]{0:T(128)S(1)} %pad_add_fusion.where, bf16[3,640,1280]{2,1,0:T(8,128)(2,1)S(1)} %arrange_latent.1.lat_ref, bf16[5,128,640]{2,1,0:T(8,128)(2,1)} %temporal_backward.1.own_ref, ...), custom_call_target="tpu_custom_call" | custom-call | flops 4718592000 | bytes 3686400 | tf_op jit(solution)/shard_map/spatial_send/pallas_call | solution.py:431
  86.2 13.9 %collective-permute-start.9 = (bf16[1152,640]{1,0:T(8,128)(2,1)}, bf16[1152,640]{1,0:T(8,128)(2,1)}, u32[]{:S(2)}, u32[]{:S(2)}) collective-permute-start(bf16[1152,640]{1,0:T(8,128)(2,1)} %bitcast.16), channel_id=1, source_target_pairs={{0,32},{1,97},{2,34},{3,99},{4,36},{5,101},{6,38},{7,103},{8,40},{... | collective-permute-start | bytes 4423688 | tf_op jit(solution)/shard_map/ppermute | solution.py:688
  102.7 11.2 %spatial_keep.1 = (f32[3,320,640]{2,1,0:T(8,128)S(1)}, f32[3,320,640]{2,1,0:T(8,128)S(1)}, f32[3,320,640]{2,1,0:T(8,128)S(1)}) custom-call(s32[4]{0:T(128)S(1)} %pad_add_fusion.2.where, bf16[3,640,1280]{2,1,0:T(8,128)(2,1)S(1)} %copy-done.4, bf16[5,128,640]{2,1,0:T(8,128)(2,1)} %temporal_backward.1.own_ref, bf16[5,128,640]{2,1,0:T(8,128)(2,1)} %collective-permute-done.6.other_ref), custom_call_target="tpu_custom_call" | custom-call | flops 4718592000 | bytes 7372800 | tf_op jit(solution)/shard_map/spatial_keep/pallas_call | solution.py:431
  113.9 3.6 %combine_0_2.1 = (bf16[560,640]{1,0:T(8,128)(2,1)}, f32[3,160,640]{2,1,0:T(8,128)S(1)}, f32[80,640]{1,0:T(8,128)S(1)}) custom-call(s32[1]{0:T(128)} %bitcast.bit_ref, bf16[1152,640]{1,0:T(8,128)(2,1)} %collective-permute-done.21.met_ref, f32[3,320,640]{2,1,0:T(8,128)S(1)} %get-tuple-element.119.sp_ref, f32[160,640]{1,0:T(8,128)S(1)} %get-tuple-element.141.tp_ref), custom_call_target="tpu_custom_call" | custom-call | bytes 4915200 | tf_op jit(solution)/shard_map/combine_0_2/pallas_call | solution.py:585
  124.8 6.6 %collective-permute-start.10 = (bf16[576,640]{1,0:T(8,128)(2,1)}, bf16[576,640]{1,0:T(8,128)(2,1)}, u32[]{:S(2)}, u32[]{:S(2)}) collective-permute-start(bf16[576,640]{1,0:T(8,128)(2,1)} %get-tuple-element.83), channel_id=1, source_target_pairs={{0,96},{1,33},{2,98},{3,35},{4,100},{5,37},{6,102},{7,39},{8,104},... | collective-permute-start | bytes 2211848 | tf_op jit(solution)/shard_map/ppermute | solution.py:688
  134.9 2.9 %collective-permute-start.23 = (bf16[288,640]{1,0:T(8,128)(2,1)S(1)}, bf16[288,640]{1,0:T(8,128)(2,1)S(1)}, u32[]{:S(2)}, u32[]{:S(2)}) collective-permute-start(bf16[288,640]{1,0:T(8,128)(2,1)S(1)} %get-tuple-element.123), channel_id=1, source_target_pairs={{0,32},{1,97},{2,34},{3,99},{4,36},{5,101},{6,38},{7,103},{8,40},{... | collective-permute-start | bytes 1105928 | tf_op jit(solution)/shard_map/ppermute | solution.py:688
  137.8 6.0 %collective-permute-done.10.met_ref = bf16[576,640]{1,0:T(8,128)(2,1)} collective-permute-done((bf16[576,640]{1,0:T(8,128)(2,1)}, bf16[576,640]{1,0:T(8,128)(2,1)}, u32[]{:S(2)}, u32[]{:S(2)}) %collective-permute-start.10) | collective-permute-done | bytes 737312 | tf_op jit(solution)/shard_map/ppermute | solution.py:688
  150.0 3.3 %collective-permute-done.11.met_ref = bf16[304,640]{1,0:T(8,128)(2,1)S(1)} collective-permute-done((bf16[304,640]{1,0:T(8,128)(2,1)S(1)}, bf16[304,640]{1,0:T(8,128)(2,1)S(1)}, u32[]{:S(2)}, u32[]{:S(2)}) %collective-permute-start.11) | collective-permute-done | bytes 389152 | tf_op jit(solution)/shard_map/ppermute | solution.py:688
  154.3 2.8 %collective-permute-done.17.met_ref = bf16[288,640]{1,0:T(8,128)(2,1)S(1)} collective-permute-done((bf16[288,640]{1,0:T(8,128)(2,1)S(1)}, bf16[288,640]{1,0:T(8,128)(2,1)S(1)}, u32[]{:S(2)}, u32[]{:S(2)}) %collective-permute-start.17) | collective-permute-done | bytes 368672 | tf_op jit(solution)/shard_map/ppermute | solution.py:688
  157.4 5.9 %collective-permute-start.18 = (bf16[176,640]{1,0:T(8,128)(2,1)S(1)}, bf16[176,640]{1,0:T(8,128)(2,1)S(1)}, u32[]{:S(2)}, u32[]{:S(2)}) collective-permute-start(bf16[176,640]{1,0:T(8,128)(2,1)S(1)} %get-tuple-element.110), channel_id=1, source_target_pairs={{0,6},{1,3},{2,4},{3,1},{4,2},{5,7},{6,0},{7,5},{8,14},{9,11},{10,... | collective-permute-start | bytes 675848 | tf_op jit(solution)/shard_map/ppermute | solution.py:688
  163.9 4.8 %collective-permute-done.25.met_ref = bf16[112,640]{1,0:T(8,128)(2,1)S(1)} collective-permute-done((bf16[112,640]{1,0:T(8,128)(2,1)S(1)}, bf16[112,640]{1,0:T(8,128)(2,1)S(1)}, u32[]{:S(2)}, u32[]{:S(2)}) %collective-permute-start.25) | collective-permute-done | bytes 143392 | tf_op jit(solution)/shard_map/ppermute | solution.py:688
  169.8 4.5 %collective-permute-done.19.met_ref = bf16[112,640]{1,0:T(8,128)(2,1)S(1)} collective-permute-done((bf16[112,640]{1,0:T(8,128)(2,1)S(1)}, bf16[112,640]{1,0:T(8,128)(2,1)S(1)}, u32[]{:S(2)}, u32[]{:S(2)}) %collective-permute-start.19) | collective-permute-done | bytes 143392 | tf_op jit(solution)/shard_map/ppermute | solution.py:688
  174.3 3.7 %collective-permute-start.20 = (f32[64,640]{1,0:T(8,128)S(1)}, f32[64,640]{1,0:T(8,128)S(1)}, u32[]{:S(2)}, u32[]{:S(2)}) collective-permute-start(f32[64,640]{1,0:T(8,128)S(1)} %get-tuple-element.117), channel_id=1, source_target_pairs={{0,96},{1,33},{2,98},{3,35},{4,100},{5,37},{6,102},{7,39},{8,104},... | collective-permute-start | bytes 491528 | tf_op jit(solution)/shard_map/ppermute | solution.py:688
  178.3 3.0 %collective-permute-done.20 = f32[64,640]{1,0:T(8,128)S(1)} collective-permute-done((f32[64,640]{1,0:T(8,128)S(1)}, f32[64,640]{1,0:T(8,128)S(1)}, u32[]{:S(2)}, u32[]{:S(2)}) %collective-permute-start.20) | collective-permute-done | bytes 163872 | tf_op jit(solution)/shard_map/ppermute | solution.py:688
  181.4 3.8 %collective-permute-done.14 = f32[80,640]{1,0:T(8,128)S(1)} collective-permute-done((f32[80,640]{1,0:T(8,128)S(1)}, f32[80,640]{1,0:T(8,128)S(1)}, u32[]{:S(2)}, u32[]{:S(2)}) %collective-permute-start.14) | collective-permute-done | bytes 204832 | tf_op jit(solution)/shard_map/ppermute | solution.py:688
  (122 shorter events, 44.1 us)
Async XLA Ops:
  26.0 9.0 %collective-permute-start.3 = (bf16[1,128,640]{2,1,0:T(8,128)(2,1)S(1)}, bf16[1,128,640]{2,1,0:T(8,128)(2,1)S(1)}, u32[]{:S(2)}, u32[]{:S(2)}) collective-permute-start(bf16[1,128,640]{2,1,0:T(8,128)(2,1)S(1)} %get-tuple-element.145), channel_id=1, source_target_pairs={{2,0},{4,2},{6,4},{8,6},{10,8},{12,10},{14,12},{16,14},{18,16},{20... | collective-permute-start | bytes 491528 | tf_op jit(solution)/shard_map/ppermute | solution.py:637
  27.3 8.6 %collective-permute-start.2 = (bf16[1,128,640]{2,1,0:T(8,128)(2,1)S(1)}, bf16[1,128,640]{2,1,0:T(8,128)(2,1)S(1)}, u32[]{:S(2)}, u32[]{:S(2)}) collective-permute-start(bf16[1,128,640]{2,1,0:T(8,128)(2,1)S(1)} %get-tuple-element.146), channel_id=1, source_target_pairs={{0,2},{2,4},{4,6},{6,8},{8,10},{10,12},{12,14},{14,16},{16,18},{18... | collective-permute-start | bytes 491528 | tf_op jit(solution)/shard_map/ppermute | solution.py:636
  34.8 24.0 %collective-permute-start = (bf16[640,640]{1,0:T(8,128)(2,1)}, bf16[640,640]{1,0:T(8,128)(2,1)}, u32[]{:S(2)}, u32[]{:S(2)}) collective-permute-start(bf16[640,640]{1,0:T(8,128)(2,1)} %get-tuple-element.71), channel_id=1, source_target_pairs={{0,1},{1,0},{2,3},{3,2},{4,5},{5,4},{6,7},{7,6},{8,9},{9,8},{10,11... | collective-permute-start | bytes 2457608 | tf_op jit(solution)/shard_map/ppermute | solution.py:639
  40.9 8.4 %collective-permute-start.5 = (bf16[1,128,640]{2,1,0:T(8,128)(2,1)S(1)}, bf16[1,128,640]{2,1,0:T(8,128)(2,1)S(1)}, u32[]{:S(2)}, u32[]{:S(2)}) collective-permute-start(bf16[1,128,640]{2,1,0:T(8,128)(2,1)S(1)} %get-tuple-element.143), channel_id=1, source_target_pairs={{2,0},{4,2},{6,4},{8,6},{10,8},{12,10},{14,12},{16,14},{18,16},{20... | collective-permute-start | bytes 491528 | tf_op jit(solution)/shard_map/ppermute | solution.py:645
  42.2 8.3 %collective-permute-start.4 = (bf16[1,128,640]{2,1,0:T(8,128)(2,1)S(1)}, bf16[1,128,640]{2,1,0:T(8,128)(2,1)S(1)}, u32[]{:S(2)}, u32[]{:S(2)}) collective-permute-start(bf16[1,128,640]{2,1,0:T(8,128)(2,1)S(1)} %get-tuple-element.144), channel_id=1, source_target_pairs={{0,2},{2,4},{4,6},{6,8},{8,10},{10,12},{12,14},{14,16},{16,18},{18... | collective-permute-start | bytes 491528 | tf_op jit(solution)/shard_map/ppermute | solution.py:644
  47.3 17.0 %collective-permute-start.8 = (bf16[5,128,640]{2,1,0:T(8,128)(2,1)}, bf16[5,128,640]{2,1,0:T(8,128)(2,1)}, u32[]{:S(2)}, u32[]{:S(2)}) collective-permute-start(bf16[5,128,640]{2,1,0:T(8,128)(2,1)} %get-tuple-element.73.gp_ref), channel_id=1, source_target_pairs={{0,1},{1,0},{2,3},{3,2},{4,5},{5,4},{6,7},{7,6},{8,9},{9,8},{10,11... | collective-permute-start | bytes 2457608 | tf_op jit(solution)/shard_map/ppermute | solution.py:646
  55.2 15.8 %collective-permute-start.6 = (bf16[5,128,640]{2,1,0:T(8,128)(2,1)}, bf16[5,128,640]{2,1,0:T(8,128)(2,1)}, u32[]{:S(2)}, u32[]{:S(2)}) collective-permute-start(bf16[5,128,640]{2,1,0:T(8,128)(2,1)} %temporal_backward.1.own_ref), channel_id=1, source_target_pairs={{0,1},{1,0},{2,3},{3,2},{4,5},{5,4},{6,7},{7,6},{8,9},{9,8},{10,11... | collective-permute-start | bytes 2457608 | tf_op jit(solution)/shard_map/ppermute | solution.py:653
  58.1 6.2 %collective-permute-start.7 = (bf16[336,896]{1,0:T(8,128)(2,1)}, bf16[336,896]{1,0:T(8,128)(2,1)}, u32[]{:S(2)}, u32[]{:S(2)}) collective-permute-start(bf16[336,896]{1,0:T(8,128)(2,1)} %get-tuple-element.77), channel_id=1, source_target_pairs={{0,1},{1,0},{2,3},{3,2},{4,5},{5,4},{6,7},{7,6},{8,9},{9,8},{10,11... | collective-permute-start | bytes 1806344 | tf_op jit(solution)/shard_map/ppermute | solution.py:650
  83.8 30.1 %collective-permute-start.21 = (bf16[1152,640]{1,0:T(8,128)(2,1)}, bf16[1152,640]{1,0:T(8,128)(2,1)}, u32[]{:S(2)}, u32[]{:S(2)}) collective-permute-start(bf16[1152,640]{1,0:T(8,128)(2,1)} %bitcast.34), channel_id=1, source_target_pairs={{0,2},{1,7},{2,0},{3,5},{4,6},{5,3},{6,4},{7,1},{8,10},{9,15},{10,... | collective-permute-start | bytes 4423688 | tf_op jit(solution)/shard_map/ppermute | solution.py:688
  86.2 32.3 %collective-permute-start.9 = (bf16[1152,640]{1,0:T(8,128)(2,1)}, bf16[1152,640]{1,0:T(8,128)(2,1)}, u32[]{:S(2)}, u32[]{:S(2)}) collective-permute-start(bf16[1152,640]{1,0:T(8,128)(2,1)} %bitcast.16), channel_id=1, source_target_pairs={{0,32},{1,97},{2,34},{3,99},{4,36},{5,101},{6,38},{7,103},{8,40},{... | collective-permute-start | bytes 4423688 | tf_op jit(solution)/shard_map/ppermute | solution.py:688
  100.1 31.3 %collective-permute-start.15 = (bf16[1152,640]{1,0:T(8,128)(2,1)}, bf16[1152,640]{1,0:T(8,128)(2,1)}, u32[]{:S(2)}, u32[]{:S(2)}) collective-permute-start(bf16[1152,640]{1,0:T(8,128)(2,1)} %bitcast.25), channel_id=1, source_target_pairs={{0,8},{1,25},{2,10},{3,27},{4,12},{5,29},{6,14},{7,31},{8,0},{9,17... | collective-permute-start | bytes 4423688 | tf_op jit(solution)/shard_map/ppermute | solution.py:688
  118.6 14.9 %collective-permute-start.22 = (bf16[560,640]{1,0:T(8,128)(2,1)}, bf16[560,640]{1,0:T(8,128)(2,1)}, u32[]{:S(2)}, u32[]{:S(2)}) collective-permute-start(bf16[560,640]{1,0:T(8,128)(2,1)} %get-tuple-element.120), channel_id=1, source_target_pairs={{0,6},{1,3},{2,4},{3,1},{4,2},{5,7},{6,0},{7,5},{8,14},{9,11},{10,... | collective-permute-start | bytes 2150408 | tf_op jit(solution)/shard_map/ppermute | solution.py:688
  124.8 19.0 %collective-permute-start.10 = (bf16[576,640]{1,0:T(8,128)(2,1)}, bf16[576,640]{1,0:T(8,128)(2,1)}, u32[]{:S(2)}, u32[]{:S(2)}) collective-permute-start(bf16[576,640]{1,0:T(8,128)(2,1)} %get-tuple-element.83), channel_id=1, source_target_pairs={{0,96},{1,33},{2,98},{3,35},{4,100},{5,37},{6,102},{7,39},{8,104},... | collective-permute-start | bytes 2211848 | tf_op jit(solution)/shard_map/ppermute | solution.py:688
  133.3 14.0 %collective-permute-start.16 = (bf16[560,640]{1,0:T(8,128)(2,1)S(1)}, bf16[560,640]{1,0:T(8,128)(2,1)S(1)}, u32[]{:S(2)}, u32[]{:S(2)}) collective-permute-start(bf16[560,640]{1,0:T(8,128)(2,1)S(1)} %get-tuple-element.104), channel_id=1, source_target_pairs={{0,24},{1,9},{2,26},{3,11},{4,28},{5,13},{6,30},{7,15},{8,16},{9,1... | collective-permute-start | bytes 2150408 | tf_op jit(solution)/shard_map/ppermute | solution.py:688
  134.9 13.0 %collective-permute-start.23 = (bf16[288,640]{1,0:T(8,128)(2,1)S(1)}, bf16[288,640]{1,0:T(8,128)(2,1)S(1)}, u32[]{:S(2)}, u32[]{:S(2)}) collective-permute-start(bf16[288,640]{1,0:T(8,128)(2,1)S(1)} %get-tuple-element.123), channel_id=1, source_target_pairs={{0,32},{1,97},{2,34},{3,99},{4,36},{5,101},{6,38},{7,103},{8,40},{... | collective-permute-start | bytes 1105928 | tf_op jit(solution)/shard_map/ppermute | solution.py:688
  145.3 7.9 %collective-permute-start.11 = (bf16[304,640]{1,0:T(8,128)(2,1)S(1)}, bf16[304,640]{1,0:T(8,128)(2,1)S(1)}, u32[]{:S(2)}, u32[]{:S(2)}) collective-permute-start(bf16[304,640]{1,0:T(8,128)(2,1)S(1)} %get-tuple-element.87), channel_id=1, source_target_pairs={{0,8},{1,25},{2,10},{3,27},{4,12},{5,29},{6,14},{7,31},{8,0},{9,17... | collective-permute-start | bytes 1167368 | tf_op jit(solution)/shard_map/ppermute | solution.py:688
  147.6 9.5 %collective-permute-start.17 = (bf16[288,640]{1,0:T(8,128)(2,1)S(1)}, bf16[288,640]{1,0:T(8,128)(2,1)S(1)}, u32[]{:S(2)}, u32[]{:S(2)}) collective-permute-start(bf16[288,640]{1,0:T(8,128)(2,1)S(1)} %get-tuple-element.107), channel_id=1, source_target_pairs={{0,2},{1,7},{2,0},{3,5},{4,6},{5,3},{6,4},{7,1},{8,10},{9,15},{10,... | collective-permute-start | bytes 1105928 | tf_op jit(solution)/shard_map/ppermute | solution.py:688
  148.3 15.1 %collective-permute-start.24 = (bf16[176,640]{1,0:T(8,128)(2,1)S(1)}, bf16[176,640]{1,0:T(8,128)(2,1)S(1)}, u32[]{:S(2)}, u32[]{:S(2)}) collective-permute-start(bf16[176,640]{1,0:T(8,128)(2,1)S(1)} %get-tuple-element.126), channel_id=1, source_target_pairs={{0,96},{1,33},{2,98},{3,35},{4,100},{5,37},{6,102},{7,39},{8,104},... | collective-permute-start | bytes 675848 | tf_op jit(solution)/shard_map/ppermute | solution.py:688
  153.6 10.0 %collective-permute-start.12 = (bf16[192,640]{1,0:T(8,128)(2,1)S(1)}, bf16[192,640]{1,0:T(8,128)(2,1)S(1)}, u32[]{:S(2)}, u32[]{:S(2)}) collective-permute-start(bf16[192,640]{1,0:T(8,128)(2,1)S(1)} %get-tuple-element.91), channel_id=1, source_target_pairs={{0,24},{1,9},{2,26},{3,11},{4,28},{5,13},{6,30},{7,15},{8,16},{9,1... | collective-permute-start | bytes 737288 | tf_op jit(solution)/shard_map/ppermute | solution.py:688
  157.4 11.4 %collective-permute-start.18 = (bf16[176,640]{1,0:T(8,128)(2,1)S(1)}, bf16[176,640]{1,0:T(8,128)(2,1)S(1)}, u32[]{:S(2)}, u32[]{:S(2)}) collective-permute-start(bf16[176,640]{1,0:T(8,128)(2,1)S(1)} %get-tuple-element.110), channel_id=1, source_target_pairs={{0,6},{1,3},{2,4},{3,1},{4,2},{5,7},{6,0},{7,5},{8,14},{9,11},{10,... | collective-permute-start | bytes 675848 | tf_op jit(solution)/shard_map/ppermute | solution.py:688
  163.8 14.2 %collective-permute-start.13 = (bf16[128,640]{1,0:T(8,128)(2,1)S(1)}, bf16[128,640]{1,0:T(8,128)(2,1)S(1)}, u32[]{:S(2)}, u32[]{:S(2)}) collective-permute-start(bf16[128,640]{1,0:T(8,128)(2,1)S(1)} %get-tuple-element.95), channel_id=1, source_target_pairs={{0,2},{1,7},{2,0},{3,5},{4,6},{5,3},{6,4},{7,1},{8,10},{9,15},{10,... | collective-permute-start | bytes 491528 | tf_op jit(solution)/shard_map/ppermute | solution.py:688
  168.8 9.5 %collective-permute-start.26 = (f32[64,640]{1,0:T(8,128)S(1)}, f32[64,640]{1,0:T(8,128)S(1)}, u32[]{:S(2)}, u32[]{:S(2)}) collective-permute-start(f32[64,640]{1,0:T(8,128)S(1)} %get-tuple-element.133), channel_id=1, source_target_pairs={{0,24},{1,9},{2,26},{3,11},{4,28},{5,13},{6,30},{7,15},{8,16},{9,1... | collective-permute-start | bytes 491528 | tf_op jit(solution)/shard_map/ppermute | solution.py:688
  174.3 7.0 %collective-permute-start.20 = (f32[64,640]{1,0:T(8,128)S(1)}, f32[64,640]{1,0:T(8,128)S(1)}, u32[]{:S(2)}, u32[]{:S(2)}) collective-permute-start(f32[64,640]{1,0:T(8,128)S(1)} %get-tuple-element.117), channel_id=1, source_target_pairs={{0,96},{1,33},{2,98},{3,35},{4,100},{5,37},{6,102},{7,39},{8,104},... | collective-permute-start | bytes 491528 | tf_op jit(solution)/shard_map/ppermute | solution.py:688
  178.1 7.0 %collective-permute-start.14 = (f32[80,640]{1,0:T(8,128)S(1)}, f32[80,640]{1,0:T(8,128)S(1)}, u32[]{:S(2)}, u32[]{:S(2)}) collective-permute-start(f32[80,640]{1,0:T(8,128)S(1)} %get-tuple-element.100), channel_id=1, source_target_pairs={{0,6},{1,3},{2,4},{3,1},{4,2},{5,7},{6,0},{7,5},{8,14},{9,11},{10,... | collective-permute-start | bytes 614408 | tf_op jit(solution)/shard_map/ppermute | solution.py:688
  (25 other events, 120.8 us)

commit v2 on v1

v2 whole, which is shorter than its diff:
```python
import functools
import math

import jax
import jax.numpy as jnp
import numpy as np
from jax import lax
from jax.experimental import pallas as pl
from jax.experimental.pallas import tpu as pltpu
from jax.sharding import PartitionSpec as P

CLIP = 80
STEPS = 1000
BF = jnp.bfloat16
F32 = jnp.float32
MIB = 1 << 20
STRIDES = (16, 4, 1)
RING = 4
ORDERS = ((0, 1, 2), (1, 2, 0), (2, 0, 1))
LOSS = 16
EXTRA = 64


def params(mib):
    return pltpu.CompilerParams(vmem_limit_bytes=mib * MIB)


def in_hbm(x):
    return pltpu.with_memory_space_constraint(x, pltpu.HBM)


def in_vmem(x):
    return pltpu.with_memory_space_constraint(x, pltpu.VMEM)


def cost(flops, nbytes):
    return pl.CostEstimate(flops=int(flops), bytes_accessed=int(nbytes), transcendentals=0)


def tap_of(step):
    group = step // 3
    return jnp.where(group == 0, 1, jnp.where(group == 1, 0, 2)), step % 3


def spatial_forward_kernel(
    odd, x_ref, above_ref, below_ref, w_ref, act_ref, one_ref, two_ref, der_ref, xp, acc, taps, sems
):
    step = pl.program_id(0)
    first, second = tap_of(step)
    frames, span, channels = x_ref.shape
    cols = above_ref.shape[1]
    features = w_ref.shape[3]

    @pl.when(step == 0)
    def _():
        for k in range(9):
            row = (1, 0, 2)[k // 3]
            pltpu.make_async_copy(w_ref.at[row, k % 3], taps.at[k], sems.at[k]).start()
        xp[:, 0:cols, :] = above_ref[...]
        xp[:, cols : cols + span, :] = x_ref[...]
        xp[:, cols + span : span + 2 * cols, :] = below_ref[...]

    pltpu.make_async_copy(w_ref.at[first, second], taps.at[step], sems.at[step]).wait()
    start = pl.multiple_of(first * cols, cols)
    piece = xp[:, pl.ds(start, span), :].reshape(frames * span, channels)
    prod = jnp.dot(piece, taps[step], preferred_element_type=F32)

    @pl.when(step < 3)
    def _():
        acc[second] = prod

    @pl.when(step >= 3)
    def _():
        acc[second] += prod

    @pl.when(step == 8)
    def _():
        col = lax.broadcasted_iota(jnp.int32, (span, features), 0) % cols

        def one(f, carry):
            rows = pl.ds(pl.multiple_of(f * span, span), span)
            left = jnp.where(col == 0, 0.0, pltpu.roll(acc[0, rows, :], 1, 0))
            right = jnp.where(col == cols - 1, 0.0, pltpu.roll(acc[2, rows, :], span - 1, 0))
            hidden = left + acc[1, rows, :] + right
            sig = 1.0 / (1.0 + jnp.exp(-hidden))
            act_ref[f] = (hidden * sig).astype(BF)
            der_ref[f] = sig * (1.0 + hidden * (1.0 - sig))
            return carry

        lax.fori_loop(0, frames, one, 0)
        one_ref[0] = act_ref[(1 - odd[0]) * (frames - 1)]
        two_ref[0] = act_ref[odd[0] * (frames - 1)]


def spatial_forward(odd, x, above, below, weight):
    frames, span, channels = x.shape
    cols = above.shape[1]
    features = weight.shape[3]
    whole = lambda s: (0, 0, 0)
    return pl.pallas_call(
        spatial_forward_kernel,
        grid=(9,),
        in_specs=[
            pl.BlockSpec(memory_space=pltpu.SMEM),
            pl.BlockSpec(x.shape, whole),
            pl.BlockSpec(above.shape, whole),
            pl.BlockSpec(below.shape, whole),
            pl.BlockSpec(memory_space=pltpu.HBM),
        ],
        out_specs=[
            pl.BlockSpec((frames, span, features), whole),
            pl.BlockSpec((1, span, features), whole),
            pl.BlockSpec((1, span, features), whole),
            pl.BlockSpec((frames, span, features), whole),
        ],
        out_shape=[
            jax.ShapeDtypeStruct((frames, span, features), BF),
            jax.ShapeDtypeStruct((1, span, features), BF),
            jax.ShapeDtypeStruct((1, span, features), BF),
            pltpu.VMEM((frames, span, features), F32),
        ],
        scratch_shapes=[
            pltpu.VMEM((frames, span + 2 * cols, channels), BF),
            pltpu.VMEM((3, frames * span, features), F32),
            pltpu.VMEM((9, channels, features), BF),
            pltpu.SemaphoreType.DMA((9,)),
        ],
        compiler_params=params(40),
        cost_estimate=cost(
            2 * 9 * frames * span * channels * features, 2 * 9 * channels * features
        ),
        name="spatial_forward",
    )(odd, x, above, below, in_hbm(weight))


def temporal_forward_kernel(
    scale, odd, act_ref, one_ref, two_ref, w_ref, clean_ref, noise_ref, *rest
):
    gp_ref, one_out, two_out, loss_ref, rim_ref, ap = rest[1:]
    frames, span, features = act_ref.shape
    factor = scale[2]
    ap[(1 - odd[0]) * (frames + 1)] = one_ref[0]
    ap[odd[0] * (frames + 1)] = two_ref[0]
    ap[1 : frames + 1] = act_ref[...]
    pred = jnp.zeros((frames * span, features), F32)
    for tap in range(3):
        pred = pred + jnp.dot(
            ap[tap : tap + frames].reshape(frames * span, features),
            w_ref[tap],
            preferred_element_type=F32,
        )
    clean = clean_ref[...].reshape(frames * span, features).astype(F32)
    noise = noise_ref[...].reshape(frames * span, features).astype(F32)
    diff = pred - (scale[0] * noise - scale[1] * clean)
    gp_ref[...] = (2.0 * diff / factor).astype(BF).reshape(frames, span, features)
    one_out[0] = gp_ref[(1 - odd[0]) * (frames - 1)]
    two_out[0] = gp_ref[odd[0] * (frames - 1)]
    loss = jnp.sum(diff * diff, axis=0, keepdims=True)
    loss_ref[...] = loss
    rim_ref[0:span, :] = ap[0]
    rim_ref[span : 2 * span, :] = ap[frames + 1]
    rim_ref[2 * span :, :] = stacked(loss, LOSS).astype(BF)


def temporal_forward(scale, odd, act, one, two, weight, clean, noise, token):
    frames, span, features = act.shape
    whole = lambda i: (0, 0, 0)
    head = pl.BlockSpec((frames, span, features), whole)
    halo = pl.BlockSpec((1, span, features), whole)
    return pl.pallas_call(
        temporal_forward_kernel,
        grid=(1,),
        in_specs=[
            pl.BlockSpec(memory_space=pltpu.SMEM),
            pl.BlockSpec(memory_space=pltpu.SMEM),
            head,
            halo,
            halo,
            pl.BlockSpec(weight.shape, whole),
            head,
            head,
            pl.BlockSpec(memory_space=pl.ANY),
        ],
        out_specs=[
            head,
            halo,
            halo,
            pl.BlockSpec((1, features), lambda i: (0, 0)),
            pl.BlockSpec((2 * span + LOSS, features), lambda i: (0, 0)),
        ],
        out_shape=[
            jax.ShapeDtypeStruct((frames, span, features), BF),
            jax.ShapeDtypeStruct((1, span, features), BF),
            jax.ShapeDtypeStruct((1, span, features), BF),
            jax.ShapeDtypeStruct((1, features), F32),
            jax.ShapeDtypeStruct((2 * span + LOSS, features), BF),
        ],
        scratch_shapes=[pltpu.VMEM((frames + 2, span, features), BF)],
        compiler_params=params(16),
        cost_estimate=cost(2 * 3 * frames * span * features * features, 6 * features * features),
        name="temporal_forward",
    )(scale, odd, act, one, two, weight, clean, noise, token)


def thirds(value):
    high = value.astype(BF)
    rest = value - high.astype(F32)
    middle = rest.astype(BF)
    return high, middle, (rest - middle.astype(F32)).astype(BF)


def stacked(value, rows):
    high, middle, low = thirds(value)
    row = lax.broadcasted_iota(jnp.int32, (rows, value.shape[1]), 0)
    parts = [p.astype(F32) for p in (high, middle, low)]
    return jnp.where(
        row == 0, parts[0], jnp.where(row == 1, parts[1], jnp.where(row == 2, parts[2], 0.0))
    )


def joined(rows):
    return (rows[0:1] + rows[1:2]) + rows[2:3]


def temporal_grad_kernel(
    bits_ref,
    act_ref,
    rim_ref,
    act_other_ref,
    rim_other_ref,
    gp_ref,
    gp_other_ref,
    choice_ref,
    reorder_ref,
    loss_ref,
    send_ref,
    keep_0,
    keep_1,
    keep_2,
    sum_ref,
    padded,
    chosen,
    gps,
    total,
):
    frames, span, features = gp_ref.shape
    core = bits_ref[3]
    half = features // 2
    rows = half // 2
    loss = loss_ref[...] + joined(rim_other_ref[2 * span : 2 * span + LOSS, :].astype(F32))
    sum_ref[...] = loss
    for which, (act, rim) in enumerate(((act_ref, rim_ref), (act_other_ref, rim_other_ref))):
        padded[which, 0] = rim[0:span, :]
        padded[which, 1 : frames + 1] = act[...]
        padded[which, frames + 1] = rim[span : 2 * span, :]
    chosen[...] = lax.dot_general(
        choice_ref[core],
        padded[...].reshape(-1, features),
        (((1,), (1,)), ((), ())),
        preferred_element_type=F32,
    ).astype(BF)
    gps[0:frames] = gp_ref[...]
    gps[frames:] = gp_other_ref[...]
    for tap, keep in enumerate((keep_0, keep_1, keep_2)):
        here = tap * span
        there = here + (frames + 2) * span
        long = frames * span
        left = jnp.concatenate(
            [chosen[:, here : here + long], chosen[:, there : there + long]], axis=1
        )
        if tap > 0:
            left = jnp.dot(
                reorder_ref[core, tap - 1], left, preferred_element_type=F32
            ).astype(BF)
        total[...] = jnp.dot(
            left, gps[...].reshape(2 * long, features), preferred_element_type=F32
        )
        bit = bits_ref[tap]
        kept = pl.ds(pl.multiple_of(bit * rows, rows), rows)
        sent = pl.ds(pl.multiple_of((1 - bit) * rows, rows), rows)
        keep[...] = total[kept, :]
        send_ref[tap, 0:rows, :] = total[sent, :].astype(BF)
        send_ref[tap, rows : rows + LOSS, :] = stacked(loss, LOSS).astype(BF)
        send_ref[tap, rows + LOSS :, :] = jnp.zeros(
            (send_ref.shape[1] - rows - LOSS, features), BF
        )


def temporal_grad_local(
    bits, act, rim, act_other, rim_other, gp, gp_other, choice, reorder, loss
):
    frames, span, features = gp.shape
    rows = features // 4
    vmem = pl.BlockSpec(memory_space=pltpu.VMEM)
    return pl.pallas_call(
        temporal_grad_kernel,
        in_specs=[pl.BlockSpec(memory_space=pltpu.SMEM)]
        + [vmem] * 9,
        out_shape=[
            pltpu.VMEM((3, 3 * EXTRA, features), BF),
            *[pltpu.HBM((rows, features), F32) for _ in range(3)],
            pltpu.VMEM((1, features), F32),
        ],
        out_specs=[vmem] * 5,
        scratch_shapes=[
            pltpu.VMEM((2, frames + 2, span, features), BF),
            pltpu.VMEM((features // 2, 2 * (frames + 2) * span), BF),
            pltpu.VMEM((2 * frames, span, features), BF),
            pltpu.VMEM((features // 2, features), F32),
        ],
        compiler_params=params(20),
        cost_estimate=cost(
            2 * 4 * frames * span * features * features, 6 * features * features
        ),
        name="temporal_grad",
    )(bits, act, rim, act_other, rim_other, gp, gp_other, choice, reorder, loss)


def temporal_backward_kernel(
    odd, gp_ref, one_ref, two_ref, w_ref, der_ref, token, out_ref, pad
):
    frames, span, features = gp_ref.shape
    pad[(1 - odd[0]) * (frames + 1)] = one_ref[0]
    pad[odd[0] * (frames + 1)] = two_ref[0]
    pad[1 : frames + 1] = gp_ref[...]
    total = jnp.zeros((frames * span, features), F32)
    for tap in range(3):
        total = total + lax.dot_general(
            pad[2 - tap : 2 - tap + frames].reshape(frames * span, features),
            w_ref[tap],
            (((1,), (1,)), ((), ())),
            preferred_element_type=F32,
        )
    der = der_ref[...].reshape(frames * span, features)
    out_ref[...] = (total * der).astype(BF).reshape(frames, span, features)


def temporal_backward(odd, gp, one, two, weight, der, token):
    frames, span, features = gp.shape
    return pl.pallas_call(
        temporal_backward_kernel,
        in_specs=[pl.BlockSpec(memory_space=pltpu.SMEM)]
        + [pl.BlockSpec(memory_space=pltpu.VMEM)] * 5
        + [pl.BlockSpec(memory_space=pl.ANY)],
        out_shape=pltpu.VMEM((frames, span, features), BF),
        scratch_shapes=[pltpu.VMEM((frames + 2, span, features), BF)],
        compiler_params=params(12),
        cost_estimate=cost(2 * 3 * frames * span * features * features, 6 * features * features),
        name="temporal_backward",
    )(odd, gp, one, two, weight, der, token)


def select_latent_kernel(core_ref, x_ref, choice_ref, token, own_ref, send_ref):
    core = core_ref[0]
    x = x_ref[...].reshape(-1, x_ref.shape[2])
    for out, which in ((send_ref, 1 - core), (own_ref, core)):
        out[...] = lax.dot_general(
            choice_ref[which], x, (((1,), (1,)), ((), ())), preferred_element_type=F32
        ).astype(BF)


def selected_latent(core, x, choice, token):
    frames, span, channels = x.shape
    shape = jax.ShapeDtypeStruct((channels // 2, frames * span), BF)
    vmem = pl.BlockSpec(memory_space=pltpu.VMEM)
    return pl.pallas_call(
        select_latent_kernel,
        in_specs=[
            pl.BlockSpec(memory_space=pltpu.SMEM),
            vmem,
            vmem,
            pl.BlockSpec(memory_space=pl.ANY),
        ],
        out_specs=[vmem, vmem],
        out_shape=[shape, shape],
        compiler_params=params(16),
        cost_estimate=cost(2 * frames * span * channels * channels, 4 * channels * channels),
        name="select_latent",
    )(core, x, choice, token)


def arrange_latent_kernel(
    core_ref, own_ref, other_ref, reorder_ref, token, out_ref, reorder, sem
):
    core = core_ref[0]
    copy = pltpu.make_async_copy(reorder_ref.at[core], reorder, sem)
    copy.start()
    frames = 5
    span = own_ref.shape[1] // frames
    for f in range(frames):
        here = pl.multiple_of((2 * f + core) * span, span)
        there = pl.multiple_of((2 * f + 1 - core) * span, span)
        out_ref[0, :, pl.ds(here, span)] = own_ref[:, f * span : (f + 1) * span]
        out_ref[0, :, pl.ds(there, span)] = other_ref[:, f * span : (f + 1) * span]
    copy.wait()
    for third in range(1, 3):
        out_ref[third] = jnp.dot(
            reorder[third - 1], out_ref[0], preferred_element_type=F32
        ).astype(BF)


def arranged_latent(core, own, other, reorder, token):
    half, positions = own.shape
    vmem = pl.BlockSpec(memory_space=pltpu.VMEM)
    return pl.pallas_call(
        arrange_latent_kernel,
        in_specs=[
            pl.BlockSpec(memory_space=pltpu.SMEM),
            vmem,
            vmem,
            pl.BlockSpec(memory_space=pltpu.HBM),
            pl.BlockSpec(memory_space=pl.ANY),
        ],
        out_specs=vmem,
        out_shape=pltpu.VMEM((3, half, 2 * positions), BF),
        scratch_shapes=[pltpu.VMEM(reorder.shape[1:], BF), pltpu.SemaphoreType.DMA],
        compiler_params=params(16),
        cost_estimate=cost(8 * half * half * positions, 20 * half * positions),
        name="arrange_latent",
    )(core, own, other, in_hbm(reorder), token)


def shifted_gradient(core, own_ref, other_ref, pad):
    frames, span, features = own_ref.shape
    cols = (pad.shape[2] - 2 * span) // 2
    col = lax.broadcasted_iota(jnp.int32, (span, features), 0) % cols
    rim = jnp.zeros((cols, features), BF)

    def one(f, carry):
        for b in range(3):
            pad[b, f, 0:cols, :] = rim
            pad[b, f, cols + 2 * span : 2 * cols + 2 * span, :] = rim
        for ref, place in ((own_ref, core), (other_ref, 1 - core)):
            rows = pl.ds(pl.multiple_of(cols + place * span, cols), span)
            here = ref[f]
            wide = here.astype(F32)
            later = jnp.where(col == cols - 1, 0.0, pltpu.roll(wide, span - 1, 0))
            sooner = jnp.where(col == 0, 0.0, pltpu.roll(wide, 1, 0))
            pad[0, f, rows, :] = later.astype(BF)
            pad[1, f, rows, :] = here
            pad[2, f, rows, :] = sooner.astype(BF)
        return carry

    lax.fori_loop(0, frames, one, 0)


def gradient_rows(where, lat_ref, pad, outs):
    frames = pad.shape[1]
    cols = 16
    span = pad.shape[2] // 2 - cols
    height = lat_ref.shape[1] // 2
    for first in range(3):
        rows = pl.ds(pl.multiple_of(where[1 + first] * height, height), height)
        start = (2 - first) * cols
        for second in range(3):
            grad = pad[second, :, start : start + 2 * span, :]
            outs[first][second, 0:height, :] = jnp.dot(
                lat_ref[first, rows, :],
                grad.reshape(2 * frames * span, -1),
                preferred_element_type=F32,
            ).astype(outs[first].dtype)


def spatial_send_kernel(where, lat_ref, own_ref, other_ref, extra_ref, *outs):
    outs, pad = outs[:3], outs[3]
    shifted_gradient(where[0], own_ref, other_ref, pad)
    for first in range(3):
        for second in range(3):
            outs[first][second, lat_ref.shape[1] // 2 :, :] = extra_ref[
                first, second * EXTRA : (second + 1) * EXTRA, :
            ]
    gradient_rows(where, lat_ref, pad, outs)


def spatial_keep_kernel(where, lat_ref, own_ref, other_ref, *outs):
    outs, pad = outs[:3], outs[3]
    shifted_gradient(where[0], own_ref, other_ref, pad)
    gradient_rows(where, lat_ref, pad, outs)


def spatial_send(where, lat, own, other, extra):
    frames, span, features = own.shape
    rows = lat.shape[1] // 2
    cols = 16
    vmem = pl.BlockSpec(memory_space=pltpu.VMEM)
    return pl.pallas_call(
        spatial_send_kernel,
        in_specs=[pl.BlockSpec(memory_space=pltpu.SMEM)] + [vmem] * 4,
        out_specs=[vmem] * 3,
        out_shape=[pltpu.VMEM((3, rows + EXTRA, features), BF)] * 3,
        scratch_shapes=[pltpu.VMEM((3, frames, 2 * span + 2 * cols, features), BF)],
        compiler_params=params(24),
        cost_estimate=cost(
            2 * 9 * rows * 2 * frames * span * features, 2 * 9 * rows * features
        ),
        name="spatial_send",
    )(where, in_vmem(lat), own, other, in_vmem(extra))


def spatial_keep(where, lat, own, other):
    frames, span, features = own.shape
    rows = lat.shape[1] // 2
    cols = 16
    vmem = pl.BlockSpec(memory_space=pltpu.VMEM)
    return pl.pallas_call(
        spatial_keep_kernel,
        in_specs=[pl.BlockSpec(memory_space=pltpu.SMEM)]
        + [vmem] * 3,
        out_specs=[vmem] * 3,
        out_shape=[pltpu.HBM((3, rows, features), F32)] * 3,
        scratch_shapes=[pltpu.VMEM((3, frames, 2 * span + 2 * cols, features), BF)],
        compiler_params=params(24),
        cost_estimate=cost(1, 1),
        name="spatial_keep",
    )(where, in_vmem(lat), own, other)


def bit_of(value, kind):
    if kind == 0:
        return value // 2
    return (value + 1) // 2 % 2


def swap_pairs(axis, step, size):
    pairs = []
    stride = STRIDES[axis]
    for device in range(size):
        tm, core = divmod(device, 2)
        value = tm // stride % RING
        partner = (value ^ 1) if (step + core) % 2 == 0 else (RING - 1 - value)
        pairs.append((device, (tm + (partner - value) * stride) * 2 + core))
    return pairs


def owners(order, core):
    found = []
    for n in range(RING**3):
        place = 0
        for k, axis in enumerate(order):
            digit = n // RING ** (2 - k) % RING
            first, second = divmod(digit, 2)
            low, high = (second, first) if core == 0 else (first, second)
            value = 2 * low + (low ^ high)
            place += value * STRIDES[axis]
        found.append(2 * place + core)
    return np.array(found)


def one_hot(rows, width):
    return (rows[:, None] == np.arange(width)[None, :]).astype(np.float32)


def selections(channels):
    each = channels // (2 * RING**3)
    return np.stack(
        [
            one_hot((owners(ORDERS[0], c)[:, None] * each + np.arange(each)).reshape(-1), channels)
            for c in range(2)
        ]
    )


def reorders(channels):
    each = channels // (2 * RING**3)
    found = []
    for c in range(2):
        base = list(owners(ORDERS[0], c))
        for order in ORDERS[1:]:
            at = np.array([base.index(o) for o in owners(order, c)])
            rows = (at[:, None] * each + np.arange(each)).reshape(-1)
            found.append(one_hot(rows, channels // 2))
    return np.stack(found).reshape(2, 2, channels // 2, channels // 2)


def up_to(n, multiple):
    return -(-n // multiple) * multiple


def payload_rows(rows, more, has_loss):
    return 3 * up_to(rows, 16) + (LOSS if has_loss else 0) + up_to(more, 16)


def places(rows, has_loss):
    slab = up_to(rows, 16)
    return [0, slab, 2 * slab], 3 * slab, 3 * slab + (LOSS if has_loss else 0)


def halve(ref, bit, count, send_ref, send_at):
    part = count // 2
    sent = up_to(part, 16)
    kept = up_to(part, 8)
    if part % 16 == 0:
        mine = ref[pl.ds(pl.multiple_of(bit * part, part), part), :]
        theirs = ref[pl.ds(pl.multiple_of((1 - bit) * part, part), part), :]
    else:
        whole = ref[...]
        tall = whole.shape[0]
        mine = pltpu.roll(whole, (tall - bit * part) % tall, 0)[:kept]
        theirs = pltpu.roll(whole, (tall - (1 - bit) * part) % tall, 0)[:sent]
    send_ref[send_at : send_at + sent, :] = theirs.astype(send_ref.dtype)
    return mine


def combine_early_kernel(step, has_loss, bits, *refs):
    refs = list(refs)
    keep_ref, mets = refs[0], refs[1 : 2 + step]
    refs = refs[2 + step :]
    tp_ref = refs.pop(0)
    loss_ref = refs.pop(0) if has_loss else None
    send_ref = refs.pop(0)
    sp_out = refs.pop(0) if step == 2 else None
    tp_out = refs.pop(0)
    loss_out = refs.pop(0) if has_loss else None
    full_more = refs.pop(0)
    full = refs.pop(0) if step == 2 else None
    region, extra_buf, keep_buf, tp_buf, sems = refs
    rows = keep_ref.shape[1]
    half, quarter = rows // 2, rows // 4
    if step == 0:
        count, offsets = half, [(1 - bits[1]) * half]
    elif step == 1:
        count = quarter
        offsets = [bits[1] * half + (1 - bits[2]) * quarter, (1 - bits[2]) * quarter]
    else:
        count = quarter
        offsets = [bits[1] * half + bits[2] * quarter, bits[2] * quarter, 0]

    at = pl.multiple_of(offsets[0], count)
    copies = [
        pltpu.make_async_copy(keep_ref.at[:, pl.ds(at, count), :], keep_buf, sems.at[0]),
        pltpu.make_async_copy(mets[0].at[:, pl.ds(at, count), :], region, sems.at[1]),
    ]
    if step == 0:
        copies += [
            pltpu.make_async_copy(mets[0].at[:, pl.ds(rows, EXTRA), :], extra_buf, sems.at[2]),
            pltpu.make_async_copy(tp_ref, tp_buf, sems.at[3]),
        ]
        tp_ref = tp_buf
    for c in copies:
        c.start()
    for c in copies:
        c.wait()

    tall = full_more.shape[0]
    if step == 0:
        extra = extra_buf[...].reshape(3 * EXTRA, keep_ref.shape[2]).astype(F32)
        arrived, met_loss = extra[:tall], extra[tall : tall + LOSS]
    else:
        extra = mets[step][3 * (rows >> step) :, :].astype(F32)
        skip = LOSS if has_loss else 0
        arrived, met_loss = extra[skip : skip + tall], extra[:LOSS]
    full_more[...] = tp_ref[...] + arrived
    slab = up_to(rows >> (step + 1), 16)
    for b in range(3):
        total = keep_buf[b] + region[b].astype(F32)
        for k in range(1, step + 1):
            here = pl.multiple_of(b * (rows >> k) + offsets[k], count)
            total = total + mets[k][pl.ds(here, count), :].astype(F32)
        if step < 2:
            send_ref[b * slab : (b + 1) * slab, :] = total.astype(BF)
        else:
            full[b] = total
            sp_out[b] = halve(full.at[b], bits[3], count, send_ref, b * slab)
    behind = 3 * slab
    if has_loss:
        loss = loss_ref[...] + joined(met_loss)
        loss_out[...] = loss
        send_ref[behind : behind + LOSS, :] = stacked(loss, LOSS).astype(BF)
        behind += LOSS
    tp_out[...] = halve(full_more, bits[step + 1], 2 * (rows // 4 >> step), send_ref, behind)


def combine_early(step, bits, keep, mets, tp, loss, name):
    has_loss = loss is not None
    rows, width = keep.shape[1:]
    more = rows // 2 >> step
    half = rows >> (step + 1)
    vmem = pl.BlockSpec(memory_space=pltpu.VMEM)
    hbm = pl.BlockSpec(memory_space=pltpu.HBM)
    out_shape = [pltpu.VMEM((payload_rows(half, more // 2, has_loss), width), BF)]
    if step == 2:
        out_shape.append(pltpu.VMEM((3, up_to(half, 8), width), F32))
    out_shape.append(pltpu.VMEM((up_to(more // 2, 8), width), F32))
    if has_loss:
        out_shape.append(pltpu.VMEM((1, width), F32))
    scratch = [pltpu.VMEM((more, width), F32)]
    if step == 2:
        scratch.append(pltpu.VMEM((3, rows // 4, width), F32))
    scratch += [
        pltpu.VMEM((3, rows // 2 if step == 0 else rows // 4, width), BF),
        pltpu.VMEM((3, EXTRA, width), BF),
        pltpu.VMEM((3, rows // 2 if step == 0 else rows // 4, width), F32),
        pltpu.VMEM((rows // 2, width), F32),
        pltpu.SemaphoreType.DMA((4,)),
    ]
    done = list(
        pl.pallas_call(
            functools.partial(combine_early_kernel, step, has_loss),
            in_specs=[
                pl.BlockSpec(memory_space=pltpu.SMEM),
                hbm,
                hbm,
            ]
            + [vmem] * (len(mets) - 1)
            + [hbm if step == 0 else vmem]
            + [vmem] * has_loss,
            out_specs=[vmem] * len(out_shape),
            out_shape=out_shape,
            scratch_shapes=scratch,
            compiler_params=params(12),
            cost_estimate=cost(0, 8 * rows * width),
            name=name,
        )(
            bits,
            in_hbm(keep),
            in_hbm(mets[0]),
            *[in_vmem(x) for x in mets[1:]],
            in_hbm(tp) if step == 0 else in_vmem(tp),
            *([in_vmem(loss)] if has_loss else []),
        )
    )
    send = done.pop(0)
    sp = done.pop(0) if step == 2 else None
    tp = done.pop(0)
    return send, sp, tp, (done.pop(0) if has_loss else None)


def combine_kernel(rows, more, has_loss, bit_ref, met_ref, sp_ref, tp_ref, *rest):
    if has_loss:
        loss_ref, send_ref, sp_out, tp_out, loss_out, full, full_more = rest
    else:
        send_ref, sp_out, tp_out, full, full_more = rest
    bit = bit_ref[0]
    slabs, loss_at, behind = places(rows, has_loss)
    next_slab = up_to(rows // 2, 16)
    for b in range(3):
        tall = full.shape[1]
        full[b] = sp_ref[b] + met_ref[slabs[b] : slabs[b] + tall, :].astype(F32)
        sp_out[b] = halve(full.at[b], bit, rows, send_ref, b * next_slab)
    tall = full_more.shape[0]
    full_more[...] = tp_ref[...] + met_ref[behind : behind + tall, :].astype(F32)
    behind = 3 * next_slab
    if has_loss:
        loss = loss_ref[...] + joined(met_ref[loss_at : loss_at + LOSS, :].astype(F32))
        loss_out[...] = loss
        send_ref[behind : behind + LOSS, :] = stacked(loss, LOSS).astype(send_ref.dtype)
        behind += LOSS
    tp_out[...] = halve(full_more, bit, more, send_ref, behind)


def combine(bit, met, sp, tp, loss, rows, more, name):
    has_loss = loss is not None
    width = met.shape[1]
    out_shape = [
        pltpu.VMEM((payload_rows(rows // 2, more // 2, has_loss), width), BF),
        pltpu.VMEM((3, up_to(rows // 2, 8), width), F32),
        pltpu.VMEM((up_to(more // 2, 8), width), F32),
    ]
    operands = [bit, in_vmem(met), in_vmem(sp), in_vmem(tp)]
    if has_loss:
        out_shape.append(pltpu.VMEM((1, width), F32))
        operands.append(in_vmem(loss))
    vmem = pl.BlockSpec(memory_space=pltpu.VMEM)
    done = pl.pallas_call(
        functools.partial(combine_kernel, rows, more, has_loss),
        in_specs=[pl.BlockSpec(memory_space=pltpu.SMEM)] + [vmem] * (len(operands) - 1),
        out_specs=[vmem] * len(out_shape),
        out_shape=out_shape,
        scratch_shapes=[pltpu.VMEM(sp.shape, F32), pltpu.VMEM(tp.shape, F32)],
        compiler_params=params(12),
        cost_estimate=cost(0, 8 * sp.size),
        name=name,
    )(*operands)
    return done if has_loss else (*done, None)


def on_device(clean, noise, timestep, spatial_weight, temporal_weight):
    frames, rows, cols, channels = clean.shape
    features = temporal_weight.shape[0]
    span = rows * cols
    blocks = lax.axis_size("tm")
    size = 2 * blocks
    tm = lax.axis_index("tm")
    core = lax.axis_index("space")
    both = ("tm", "space")
    step_value = timestep[0].astype(F32)
    angle = math.pi / 2.0 * (step_value + 1.0) / (STEPS + 1.0)
    signal = jnp.cos(angle)
    sigma = jnp.sin(angle)
    positions = frames * blocks * rows * 2 * cols
    scale = jnp.stack([signal, sigma, jnp.float32(math.sqrt(positions))])
    w_spatial = jnp.transpose(spatial_weight, (1, 2, 0, 3))
    w_temporal = jnp.transpose(temporal_weight, (1, 0, 2))

    def mix(c, n):
        return (signal * c.astype(F32) + sigma * n.astype(F32)).astype(BF)

    edge_at = (1 - core) * (rows - 1)
    edge = mix(
        lax.dynamic_slice_in_dim(clean, edge_at, 1, axis=1),
        lax.dynamic_slice_in_dim(noise, edge_at, 1, axis=1),
    )
    met = lax.ppermute(edge, "space", [(0, 1), (1, 0)]).reshape(frames, cols, channels)
    above = jnp.where(core == 0, jnp.zeros_like(met), met)
    below = jnp.where(core == 0, met, jnp.zeros_like(met))
    noisy = mix(clean, noise).reshape(frames, span, channels)
    cross = [(0, 1), (1, 0)]
    core_index = jnp.reshape(core, (1,)).astype(jnp.int32)
    odd = jnp.reshape(tm % 2, (1,)).astype(jnp.int32)
    act, act_one, act_two, der = spatial_forward(odd, noisy, above, below, w_spatial)

    per_clip = CLIP // frames
    shift = CLIP // 4 // frames
    swaps = []
    for low in range(2):
        pairs = [(i, i + 1) for i in range(low, blocks - 1, 2) if (i + 1 + shift) % per_clip != 0]
        swaps.append(pairs + [(j, i) for i, j in pairs])
    act_one = lax.ppermute(act_one, "tm", swaps[0])
    act_two = lax.ppermute(act_two, "tm", swaps[1])
    act_other = lax.ppermute(act, "space", cross)
    lat_own, lat_send = selected_latent(
        core_index, noisy, jnp.asarray(selections(channels), BF), der
    )
    lat_other = lax.ppermute(lat_send, "space", cross)
    flat = (frames, span, channels)
    gp, gp_one, gp_two, loss_lanes, rim = temporal_forward(
        scale,
        odd,
        act,
        act_one,
        act_two,
        w_temporal,
        clean.reshape(flat),
        noise.reshape(flat),
        lat_own,
    )
    gp_one = lax.ppermute(gp_one, "tm", swaps[0])
    gp_two = lax.ppermute(gp_two, "tm", swaps[1])
    gp_other = lax.ppermute(gp, "space", cross)
    rim_other = lax.ppermute(rim, "space", cross)
    bits = []
    for order in ORDERS:
        own = []
        for axis in order:
            value = tm // STRIDES[axis] % RING
            low, high = bit_of(value, 0), bit_of(value, 1)
            own.append(jnp.where(core == 0, high, low))
            own.append(jnp.where(core == 0, low, high))
        bits.append([b.astype(jnp.int32) for b in own])
    first_bits = jnp.stack([b[0] for b in bits])
    extra, *more_keeps, loss = temporal_grad_local(
        jnp.concatenate([first_bits, core_index]),
        act,
        rim,
        act_other,
        rim_other,
        gp,
        gp_other,
        jnp.asarray(selections(features), BF),
        jnp.asarray(reorders(features), BF),
        loss_lanes,
    )
    gh = temporal_backward(odd, gp, gp_one, gp_two, w_temporal, der, loss)
    gh_other = lax.ppermute(gh, "space", cross)
    lat = arranged_latent(
        core_index, lat_own, lat_other, jnp.asarray(reorders(channels), BF), gh
    )
    sends = spatial_send(
        jnp.concatenate([core_index, 1 - first_bits]), lat, gh, gh_other, extra
    )
    keeps = spatial_keep(jnp.concatenate([core_index, first_bits]), lat, gh, gh_other)

    state = [
        (sends[t].reshape(-1, features), None, more_keeps[t], loss if t == 0 else None)
        for t in range(3)
    ]
    arrived = [[], [], []]
    count, more = channels // 4, features // 4
    for step in range(6):
        met = [
            lax.ppermute(state[t][0], both, swap_pairs(ORDERS[t][step // 2], step, size))
            for t in range(3)
        ]
        if step == 5:
            break
        for t in range(3):
            _, sp, tp, total = state[t]
            name = "combine_%d_%d" % (step, t)
            if step < 3:
                arrived[t].append(met[t].reshape(sends[t].shape) if step == 0 else met[t])
                state[t] = combine_early(
                    step, jnp.stack(bits[t]), keeps[t], arrived[t], tp, total, name
                )
            else:
                bit = jnp.reshape(bits[t][step + 1], (1,))
                state[t] = combine(bit, met[t], sp, tp, total, count, more, name)
        count, more = count // 2, more // 2

    spatial_parts, temporal_parts = [], []
    for t in range(3):
        _, sp, tp, total = state[t]
        slabs, loss_at, behind = places(count, total is not None)
        spatial_parts.append(
            jnp.stack(
                [sp[b, :count] + met[t][s : s + count].astype(F32) for b, s in enumerate(slabs)]
            )
        )
        temporal_parts.append(tp[:more] + met[t][behind : behind + more].astype(F32))
        if total is not None:
            loss_sum = jnp.sum(total + joined(met[t][loss_at : loss_at + LOSS].astype(F32)))
    spatial_grad = jnp.transpose(jnp.stack(spatial_parts), (2, 0, 1, 3))
    temporal_grad = jnp.transpose(jnp.stack(temporal_parts), (1, 0, 2))
    return (loss_sum / (positions * features), spatial_grad, temporal_grad)


def solution(mesh):
    placed = (P("tm", "space", None, None), P("tm", "space", None, None), P(), P(), P())
    return jax.shard_map(
        on_device,
        mesh=mesh,
        in_specs=placed,
        out_specs=(P(), P(("tm", "space"), None, None, None), P(("tm", "space"), None, None)),
        check_vma=False,
    )
```

time: 190 us -> 170 us (0.89)
  waiting for transfers between devices: 34.2 us -> 17.7 us
  local copies, waits for them, and re-layouts: 16.7 us -> 10.8 us
  Pallas kernels: 77.2 us -> 79.7 us
    ppermute x18, waiting for transfers between devices: 30.1 us -> 17.6 us  [on_device(): lax.ppermute(state[t][0], both, swap_pairs(ORDERS[t][step // 2], step, si...]
    unnamed x46 -> x40, local copies, waits for them, and re-layouts: 15.6 us -> 10.6 us
    ppermute x5 -> x6, waiting for transfers between devices: 4.1 us -> 0.02 us  [the longest x1 0.01 us: on_device(): act_one = lax.ppermute(act_one, 'tm', swaps[0])]
    ppermute x5 -> x6, starting transfers between devices: 12.7 us -> 8.86 us  [the longest x1 4.78 us: on_device(): gp_one = lax.ppermute(gp_one, 'tm', swaps[0])]
    ppermute x18, starting transfers between devices: 39.4 us -> 42.2 us  [on_device(): lax.ppermute(state[t][0], both, swap_pairs(ORDERS[t][step // 2], step, si...]
    pallas_call x1, Pallas kernels: 15.6 us -> 18.3 us  [spatial_forward(): pl.pallas_call(spatial_forward_kernel, grid=(9,), in_specs=[pl.BlockSpec(...]
    pallas_call x20 -> x19, Pallas kernels: 48.3 us -> 47 us  [the longest x9 20.6 us: combine_early(): pl.pallas_call(functools.partial(combine_early_kernel, step, has_loss), i...]
  transfers between devices with their start and end apart: 27 -> 28, of which waited for: 11 -> 7; matrix products, arithmetic and copies ran while one was open for 2% -> 2% of each run, Pallas kernels for 26% -> 31%
where the time goes in v2:
time: 170 us; the launch traced here: 169 us
  Pallas kernels  79.7 us (47%)
  starting transfers between devices  52 us (31%)
  waiting for transfers between devices  17.7 us (10%)
  local copies, waits for them, and re-layouts  10.8 us (6%)
  other arithmetic  4.81 us (3%)
  between operations  3.7 us (2%)
    ppermute x18, starting transfers between devices, on_device(): lax.ppermute(state[t][0], both, swap_pairs(ORDERS[t][step // 2], step, si...  42.2 us
    pallas_call x9, Pallas kernels, combine_early(): pl.pallas_call(functools.partial(combine_early_kernel, step, has_loss), i...  20.6 us
    pallas_call x1, Pallas kernels, spatial_forward(): pl.pallas_call(spatial_forward_kernel, grid=(9,), in_specs=[pl.BlockSpec(...  18.3 us
    ppermute x18, waiting for transfers between devices, on_device(): lax.ppermute(state[t][0], both, swap_pairs(ORDERS[t][step // 2], step, si...  17.6 us
    unnamed x40, local copies, waits for them, and re-layouts  10.6 us
    pallas_call x1, Pallas kernels, spatial_send(): pl.pallas_call(spatial_send_kernel, in_specs=[pl.BlockSpec(memory_space=p...  9.71 us
    pallas_call x1, Pallas kernels, spatial_keep(): pl.pallas_call(spatial_keep_kernel, in_specs=[pl.BlockSpec(memory_space=p...  9.08 us
    pallas_call x1, Pallas kernels, temporal_grad_local(): pl.pallas_call(temporal_grad_kernel, in_specs=[pl.BlockSpec(memory_space=...  6.84 us
  transfers between devices with their start and end apart: 28, of which 7 were waited for; matrix products, arithmetic and copies ran while one was open for 2% of the time, Pallas kernels for 31%

profile of v2, /device:TPU:0, one launch (start us, length us, event | category | flops | bytes accessed | tf_op | source)
XLA Modules:
  0.0 168.8 jit_solution(5593781545802514193)
XLA Ops:
  2.6 2.5 %add_convert_fusion = bf16[5,8,16,1280]{3,2,1,0:T(8,128)(2,1)S(1)} fusion(bf16[5,8,16,1280]{3,2,1,0:T(8,128)(2,1)} %param.10, bf16[5,8,16,1280]{3,2,1,0:T(8,128)(2,1)} %param.9, f32[]{:T(128)} %bitcast.8, f32[]{:T(128)} %bitcast.7), kind=kLoop, calls=%fused_computation | loop fusion | flops 4915200 | bytes 4915208 | tf_op jit(solution)/shard_map/convert_element_type | solution.py:796
  5.3 18.3 %spatial_forward.1 = (bf16[5,128,640]{2,1,0:T(8,128)(2,1)}, bf16[1,128,640]{2,1,0:T(8,128)(2,1)S(1)}, bf16[1,128,640]{2,1,0:T(8,128)(2,1)S(1)}, f32[5,128,640]{2,1,0:T(8,128)S(1)}) custom-call(s32[1]{0:T(128)} %bitcast.10.odd, bf16[5,128,1280]{2,1,0:T(8,128)(2,1)S(1)} %bitcast.103, bf16[5,16,1280]{2,1,0:T(8,128)(2,1)S(1)} %get-tuple-element.148.above_ref, ...), custom_call_target="tpu_custom_call" | custom-call | flops 9437184000 | bytes 14745600 | tf_op jit(solution)/shard_map/spatial_forward/pallas_call | solution.py:100
  28.1 2.7 %select_latent.1 = (bf16[640,640]{1,0:T(8,128)(2,1)S(1)}, bf16[640,640]{1,0:T(8,128)(2,1)S(1)}) custom-call(s32[1]{0:T(128)} %bitcast.6.core_ref, bf16[5,128,1280]{2,1,0:T(8,128)(2,1)S(1)} %bitcast.104, bf16[2,640,1280]{2,1,0:T(8,128)(2,1)S(1)} %copy-done.15, f32[5,128,640]{2,1,0:T(8,128)S(1)} %get-tuple-element.69.token.der_ref), custom_call_target="tpu_custom_call" | custom-call | flops 2097152000 | bytes 6553600 | tf_op jit(solution)/shard_map/select_latent/pallas_call | solution.py:366
  31.0 4.9 %temporal_forward.1 = (bf16[5,128,640]{2,1,0:T(8,128)(2,1)S(1)}, bf16[1,128,640]{2,1,0:T(8,128)(2,1)S(1)}, bf16[1,128,640]{2,1,0:T(8,128)(2,1)S(1)}, f32[1,640]{1,0:T(1,128)S(1)}, bf16[272,640]{1,0:T(8,128)(2,1)}) custom-call(f32[3]{0:T(128)S(1)} %pad_maximum_fusion.scale, s32[1]{0:T(128)} %bitcast.10.odd, bf16[5,128,640]{2,1,0:T(8,128)(2,1)} %get-tuple-element.72.act_ref, ...), custom_call_target="tpu_custom_call" | custom-call | flops 1572864000 | bytes 2457600 | tf_op jit(solution)/shard_map/temporal_forward/pallas_call | solution.py:170
  37.5 4.8 %collective-permute-start.4 = (bf16[1,128,640]{2,1,0:T(8,128)(2,1)}, bf16[1,128,640]{2,1,0:T(8,128)(2,1)S(1)}, u32[]{:S(2)}, u32[]{:S(2)}) collective-permute-start(bf16[1,128,640]{2,1,0:T(8,128)(2,1)} %copy-done.14), channel_id=1, source_target_pairs={{0,2},{4,6},{8,10},{12,14},{16,18},{20,22},{24,26},{28,30},{32,34}... | collective-permute-start | bytes 491528 | tf_op jit(solution)/shard_map/ppermute | solution.py:837
  45.5 6.8 %temporal_grad.1 = (bf16[3,192,640]{2,1,0:T(8,128)(2,1)S(1)}, f32[160,640]{1,0:T(8,128)}, f32[160,640]{1,0:T(8,128)}, f32[160,640]{1,0:T(8,128)}, f32[1,640]{1,0:T(1,128)S(1)}) custom-call(s32[4]{0:T(128)S(1)} %pad_add_fusion.1.bits_ref, bf16[5,128,640]{2,1,0:T(8,128)(2,1)} %get-tuple-element.72.act_ref, bf16[272,640]{1,0:T(8,128)(2,1)} %get-tuple-element.78.rim_ref, ...), custom_call_target="tpu_custom_call" | custom-call | flops 2097152000 | bytes 2457600 | tf_op jit(solution)/shard_map/temporal_grad/pallas_call | solution.py:295
  53.5 2.4 %temporal_backward.1.token.own_ref = bf16[5,128,640]{2,1,0:T(8,128)(2,1)S(1)} custom-call(s32[1]{0:T(128)} %bitcast.10.odd, bf16[5,128,640]{2,1,0:T(8,128)(2,1)S(1)} %copy-done.12, bf16[1,128,640]{2,1,0:T(8,128)(2,1)S(1)} %collective-permute-done.4.one_ref, bf16[1,128,640]{2,1,0:T(8,128)(2,1)S(1)} %collective-permute-done.5.two_ref, ...), custom_call_target="tpu_custom_call" | custom-call | flops 1572864000 | bytes 2457600 | tf_op jit(solution)/shard_map/temporal_backward/pallas_call | solution.py:340
  56.3 4.4 %arrange_latent.1.lat_ref = bf16[3,640,1280]{2,1,0:T(8,128)(2,1)S(1)} custom-call(s32[1]{0:T(128)} %bitcast.6.core_ref, bf16[640,640]{1,0:T(8,128)(2,1)S(1)} %copy-done.6, bf16[640,640]{1,0:T(8,128)(2,1)S(1)} %collective-permute-done.1.other_ref, bf16[2,2,640,640]{3,2,1,0:T(8,128)(2,1)} %constant.219.clone.reorder_ref, ...), custom_call_target="tpu_custom_call" | custom-call | flops 2097152000 | bytes 8192000 | tf_op jit(solution)/shard_map/arrange_latent/pallas_call | solution.py:405
  60.8 9.7 %spatial_send.1 = (bf16[3,384,640]{2,1,0:T(8,128)(2,1)}, bf16[3,384,640]{2,1,0:T(8,128)(2,1)}, bf16[3,384,640]{2,1,0:T(8,128)(2,1)}) custom-call(s32[4]{0:T(128)S(1)} %pad_add_fusion.2.where, bf16[3,640,1280]{2,1,0:T(8,128)(2,1)S(1)} %arrange_latent.1.lat_ref, bf16[5,128,640]{2,1,0:T(8,128)(2,1)S(1)} %temporal_backward.1.token.own_ref, ...), custom_call_target="tpu_custom_call" | custom-call | flops 4718592000 | bytes 3686400 | tf_op jit(solution)/shard_map/spatial_send/pallas_call | solution.py:486
  70.5 7.5 %collective-permute-start.16 = (bf16[1152,640]{1,0:T(8,128)(2,1)}, bf16[1152,640]{1,0:T(8,128)(2,1)S(1)}, u32[]{:S(2)}, u32[]{:S(2)}) collective-permute-start(bf16[1152,640]{1,0:T(8,128)(2,1)} %bitcast.26), channel_id=1, source_target_pairs={{0,8},{1,25},{2,10},{3,27},{4,12},{5,29},{6,14},{7,31},{8,0},{9,17... | collective-permute-start | bytes 4423688 | tf_op jit(solution)/shard_map/ppermute | solution.py:881
  78.0 4.9 %collective-permute-start.10 = (bf16[1152,640]{1,0:T(8,128)(2,1)}, bf16[1152,640]{1,0:T(8,128)(2,1)}, u32[]{:S(2)}, u32[]{:S(2)}) collective-permute-start(bf16[1152,640]{1,0:T(8,128)(2,1)} %bitcast.17), channel_id=1, source_target_pairs={{0,32},{1,97},{2,34},{3,99},{4,36},{5,101},{6,38},{7,103},{8,40},{... | collective-permute-start | bytes 4423688 | tf_op jit(solution)/shard_map/ppermute | solution.py:881
  83.1 2.4 %copy-done.1 = bf16[3,640,1280]{2,1,0:T(8,128)(2,1)S(1)} copy-done((bf16[3,640,1280]{2,1,0:T(8,128)(2,1)S(1)}, bf16[3,640,1280]{2,1,0:T(8,128)(2,1)}, u32[]{:S(2)}) %copy-start.1) | copy-done | bytes 4915224
  85.5 9.1 %spatial_keep.1 = (f32[3,320,640]{2,1,0:T(8,128)}, f32[3,320,640]{2,1,0:T(8,128)}, f32[3,320,640]{2,1,0:T(8,128)}) custom-call(s32[4]{0:T(128)S(1)} %pad_add_fusion.where, bf16[3,640,1280]{2,1,0:T(8,128)(2,1)S(1)} %copy-done.1, bf16[5,128,640]{2,1,0:T(8,128)(2,1)S(1)} %temporal_backward.1.token.own_ref, bf16[5,128,640]{2,1,0:T(8,128)(2,1)S(1)} %collective-permute-done.9.other_ref), custom_call_target="tpu_custom_call" | custom-call | flops 1 | bytes 1 | tf_op jit(solution)/shard_map/spatial_keep/pallas_call | solution.py:505
  96.6 2.5 %combine_0_1.1 = (bf16[560,640]{1,0:T(8,128)(2,1)S(1)}, f32[80,640]{1,0:T(8,128)S(1)}) custom-call(s32[6]{0:T(128)S(1)} %stack.70.bits, f32[3,320,640]{2,1,0:T(8,128)} %get-tuple-element.102.refs_0_, bf16[3,384,640]{2,1,0:T(8,128)(2,1)} %bitcast.105, f32[160,640]{1,0:T(8,128)} %get-tuple-element.104.refs_2_), custom_call_target="tpu_custom_call" | custom-call | bytes 1638400 | tf_op jit(solution)/shard_map/combine_0_1/pallas_call | solution.py:697
  101.5 3.4 %combine_0_2.1 = (bf16[560,640]{1,0:T(8,128)(2,1)}, f32[80,640]{1,0:T(8,128)S(1)}) custom-call(s32[6]{0:T(128)S(1)} %stack.76.bits, f32[3,320,640]{2,1,0:T(8,128)} %get-tuple-element.117.refs_0_, bf16[3,384,640]{2,1,0:T(8,128)(2,1)} %bitcast.36.refs_1_, f32[160,640]{1,0:T(8,128)} %get-tuple-element.119.refs_2_), custom_call_target="tpu_custom_call" | custom-call | bytes 1638400 | tf_op jit(solution)/shard_map/combine_0_2/pallas_call | solution.py:697
  104.9 4.9 %collective-permute-start.23 = (bf16[560,640]{1,0:T(8,128)(2,1)}, bf16[560,640]{1,0:T(8,128)(2,1)S(1)}, u32[]{:S(2)}, u32[]{:S(2)}) collective-permute-start(bf16[560,640]{1,0:T(8,128)(2,1)} %get-tuple-element.120), channel_id=1, source_target_pairs={{0,6},{1,3},{2,4},{3,1},{4,2},{5,7},{6,0},{7,5},{8,14},{9,11},{10,... | collective-permute-start | bytes 2150408 | tf_op jit(solution)/shard_map/ppermute | solution.py:881
  109.9 2.5 %combine_0_0.1 = (bf16[576,640]{1,0:T(8,128)(2,1)S(1)}, f32[80,640]{1,0:T(8,128)S(1)}, f32[1,640]{1,0:T(1,128)S(1)}) custom-call(s32[6]{0:T(128)S(1)} %stack.62.bits, f32[3,320,640]{2,1,0:T(8,128)} %get-tuple-element.81.refs_0_, bf16[3,384,640]{2,1,0:T(8,128)(2,1)} %bitcast.18.refs_1_, f32[160,640]{1,0:T(8,128)} %get-tuple-element.84.refs_2_, ...), custom_call_target="tpu_custom_call" | custom-call | bytes 1638400 | tf_op jit(solution)/shard_map/combine_0_0/pallas_call | solution.py:697
  115.7 5.6 %collective-permute-done.23.refs_2_ = bf16[560,640]{1,0:T(8,128)(2,1)S(1)} collective-permute-done((bf16[560,640]{1,0:T(8,128)(2,1)}, bf16[560,640]{1,0:T(8,128)(2,1)S(1)}, u32[]{:S(2)}, u32[]{:S(2)}) %collective-permute-start.23) | collective-permute-done | bytes 716832 | tf_op jit(solution)/shard_map/ppermute | solution.py:881
  133.5 3.0 %collective-permute-start.25 = (bf16[176,640]{1,0:T(8,128)(2,1)S(1)}, bf16[176,640]{1,0:T(8,128)(2,1)S(1)}, u32[]{:S(2)}, u32[]{:S(2)}) collective-permute-start(bf16[176,640]{1,0:T(8,128)(2,1)S(1)} %get-tuple-element.124), channel_id=1, source_target_pairs={{0,96},{1,33},{2,98},{3,35},{4,100},{5,37},{6,102},{7,39},{8,104},... | collective-permute-start | bytes 675848 | tf_op jit(solution)/shard_map/ppermute | solution.py:881
  138.7 6.2 %collective-permute-start.13 = (bf16[192,640]{1,0:T(8,128)(2,1)S(1)}, bf16[192,640]{1,0:T(8,128)(2,1)S(1)}, u32[]{:S(2)}, u32[]{:S(2)}) collective-permute-start(bf16[192,640]{1,0:T(8,128)(2,1)S(1)} %get-tuple-element.91), channel_id=1, source_target_pairs={{0,24},{1,9},{2,26},{3,11},{4,28},{5,13},{6,30},{7,15},{8,16},{9,1... | collective-permute-start | bytes 737288 | tf_op jit(solution)/shard_map/ppermute | solution.py:881
  146.8 3.4 %collective-permute-done.20.met_ref = bf16[112,640]{1,0:T(8,128)(2,1)S(1)} collective-permute-done((bf16[112,640]{1,0:T(8,128)(2,1)S(1)}, bf16[112,640]{1,0:T(8,128)(2,1)S(1)}, u32[]{:S(2)}, u32[]{:S(2)}) %collective-permute-start.20) | collective-permute-done | bytes 143392 | tf_op jit(solution)/shard_map/ppermute | solution.py:881
  152.7 3.3 %collective-permute-done.21 = bf16[64,640]{1,0:T(8,128)(2,1)S(1)} collective-permute-done((bf16[64,640]{1,0:T(8,128)(2,1)S(1)}, bf16[64,640]{1,0:T(8,128)(2,1)S(1)}, u32[]{:S(2)}, u32[]{:S(2)}) %collective-permute-start.21) | collective-permute-done | bytes 81952 | tf_op jit(solution)/shard_map/ppermute | solution.py:881
  156.7 5.5 %collective-permute-start.15 = (bf16[80,640]{1,0:T(8,128)(2,1)S(1)}, bf16[80,640]{1,0:T(8,128)(2,1)S(1)}, u32[]{:S(2)}, u32[]{:S(2)}) collective-permute-start(bf16[80,640]{1,0:T(8,128)(2,1)S(1)} %get-tuple-element.100), channel_id=1, source_target_pairs={{0,6},{1,3},{2,4},{3,1},{4,2},{5,7},{6,0},{7,5},{8,14},{9,11},{10,... | collective-permute-start | bytes 307208 | tf_op jit(solution)/shard_map/ppermute | solution.py:881
  162.2 2.6 %collective-permute-done.15 = bf16[80,640]{1,0:T(8,128)(2,1)S(1)} collective-permute-done((bf16[80,640]{1,0:T(8,128)(2,1)S(1)}, bf16[80,640]{1,0:T(8,128)(2,1)S(1)}, u32[]{:S(2)}, u32[]{:S(2)}) %collective-permute-start.15) | collective-permute-done | bytes 102432 | tf_op jit(solution)/shard_map/ppermute | solution.py:881
  (118 shorter events, 41.6 us)
Async XLA Ops:
  23.7 7.2 %collective-permute-start.2 = (bf16[1,128,640]{2,1,0:T(8,128)(2,1)S(1)}, bf16[1,128,640]{2,1,0:T(8,128)(2,1)S(1)}, u32[]{:S(2)}, u32[]{:S(2)}) collective-permute-start(bf16[1,128,640]{2,1,0:T(8,128)(2,1)S(1)} %get-tuple-element.73), channel_id=1, source_target_pairs={{0,2},{4,6},{8,10},{12,14},{16,18},{20,22},{24,26},{28,30},{32,34}... | collective-permute-start | bytes 491528 | tf_op jit(solution)/shard_map/ppermute | solution.py:818
  26.4 16.7 %collective-permute-start.6 = (bf16[5,128,640]{2,1,0:T(8,128)(2,1)}, bf16[5,128,640]{2,1,0:T(8,128)(2,1)}, u32[]{:S(2)}, u32[]{:S(2)}) collective-permute-start(bf16[5,128,640]{2,1,0:T(8,128)(2,1)} %get-tuple-element.72.act_ref), channel_id=1, source_target_pairs={{0,1},{1,0},{2,3},{3,2},{4,5},{5,4},{6,7},{7,6},{8,9},{9,8},{10,11... | collective-permute-start | bytes 2457608 | tf_op jit(solution)/shard_map/ppermute | solution.py:820
  36.6 6.5 %collective-permute-start.8 = (bf16[5,128,640]{2,1,0:T(8,128)(2,1)S(1)}, bf16[5,128,640]{2,1,0:T(8,128)(2,1)}, u32[]{:S(2)}, u32[]{:S(2)}) collective-permute-start(bf16[5,128,640]{2,1,0:T(8,128)(2,1)S(1)} %get-tuple-element.75.gp_ref), channel_id=1, source_target_pairs={{0,1},{1,0},{2,3},{3,2},{4,5},{5,4},{6,7},{7,6},{8,9},{9,8},{10,11... | collective-permute-start | bytes 2457608 | tf_op jit(solution)/shard_map/ppermute | solution.py:839
  36.9 5.4 %collective-permute-start.7 = (bf16[272,640]{1,0:T(8,128)(2,1)}, bf16[272,640]{1,0:T(8,128)(2,1)}, u32[]{:S(2)}, u32[]{:S(2)}) collective-permute-start(bf16[272,640]{1,0:T(8,128)(2,1)} %get-tuple-element.78.rim_ref), channel_id=1, source_target_pairs={{0,1},{1,0},{2,3},{3,2},{4,5},{5,4},{6,7},{7,6},{8,9},{9,8},{10,11... | collective-permute-start | bytes 1044488 | tf_op jit(solution)/shard_map/ppermute | solution.py:840
  37.1 19.2 %collective-permute-start.1 = (bf16[640,640]{1,0:T(8,128)(2,1)}, bf16[640,640]{1,0:T(8,128)(2,1)S(1)}, u32[]{:S(2)}, u32[]{:S(2)}) collective-permute-start(bf16[640,640]{1,0:T(8,128)(2,1)} %copy-done.13), channel_id=1, source_target_pairs={{0,1},{1,0},{2,3},{3,2},{4,5},{5,4},{6,7},{7,6},{8,9},{9,8},{10,11... | collective-permute-start | bytes 2457608 | tf_op jit(solution)/shard_map/ppermute | solution.py:824
  37.5 14.8 %collective-permute-start.4 = (bf16[1,128,640]{2,1,0:T(8,128)(2,1)}, bf16[1,128,640]{2,1,0:T(8,128)(2,1)S(1)}, u32[]{:S(2)}, u32[]{:S(2)}) collective-permute-start(bf16[1,128,640]{2,1,0:T(8,128)(2,1)} %copy-done.14), channel_id=1, source_target_pairs={{0,2},{4,6},{8,10},{12,14},{16,18},{20,22},{24,26},{28,30},{32,34}... | collective-permute-start | bytes 491528 | tf_op jit(solution)/shard_map/ppermute | solution.py:837
  42.2 10.1 %collective-permute-start.5 = (bf16[1,128,640]{2,1,0:T(8,128)(2,1)S(1)}, bf16[1,128,640]{2,1,0:T(8,128)(2,1)S(1)}, u32[]{:S(2)}, u32[]{:S(2)}) collective-permute-start(bf16[1,128,640]{2,1,0:T(8,128)(2,1)S(1)} %get-tuple-element.77), channel_id=1, source_target_pairs={{2,4},{6,8},{10,12},{14,16},{18,20},{26,28},{30,32},{34,36},{38,40... | collective-permute-start | bytes 491528 | tf_op jit(solution)/shard_map/ppermute | solution.py:838
  70.5 25.0 %collective-permute-start.16 = (bf16[1152,640]{1,0:T(8,128)(2,1)}, bf16[1152,640]{1,0:T(8,128)(2,1)S(1)}, u32[]{:S(2)}, u32[]{:S(2)}) collective-permute-start(bf16[1152,640]{1,0:T(8,128)(2,1)} %bitcast.26), channel_id=1, source_target_pairs={{0,8},{1,25},{2,10},{3,27},{4,12},{5,29},{6,14},{7,31},{8,0},{9,17... | collective-permute-start | bytes 4423688 | tf_op jit(solution)/shard_map/ppermute | solution.py:881
  78.0 23.5 %collective-permute-start.22 = (bf16[1152,640]{1,0:T(8,128)(2,1)}, bf16[1152,640]{1,0:T(8,128)(2,1)}, u32[]{:S(2)}, u32[]{:S(2)}) collective-permute-start(bf16[1152,640]{1,0:T(8,128)(2,1)} %bitcast.35), channel_id=1, source_target_pairs={{0,2},{1,7},{2,0},{3,5},{4,6},{5,3},{6,4},{7,1},{8,10},{9,15},{10,... | collective-permute-start | bytes 4423688 | tf_op jit(solution)/shard_map/ppermute | solution.py:881
  78.0 31.9 %collective-permute-start.10 = (bf16[1152,640]{1,0:T(8,128)(2,1)}, bf16[1152,640]{1,0:T(8,128)(2,1)}, u32[]{:S(2)}, u32[]{:S(2)}) collective-permute-start(bf16[1152,640]{1,0:T(8,128)(2,1)} %bitcast.17), channel_id=1, source_target_pairs={{0,32},{1,97},{2,34},{3,99},{4,36},{5,101},{6,38},{7,103},{8,40},{... | collective-permute-start | bytes 4423688 | tf_op jit(solution)/shard_map/ppermute | solution.py:881
  99.1 14.5 %collective-permute-start.17 = (bf16[560,640]{1,0:T(8,128)(2,1)S(1)}, bf16[560,640]{1,0:T(8,128)(2,1)S(1)}, u32[]{:S(2)}, u32[]{:S(2)}) collective-permute-start(bf16[560,640]{1,0:T(8,128)(2,1)S(1)} %get-tuple-element.105), channel_id=1, source_target_pairs={{0,24},{1,9},{2,26},{3,11},{4,28},{5,13},{6,30},{7,15},{8,16},{9,1... | collective-permute-start | bytes 2150408 | tf_op jit(solution)/shard_map/ppermute | solution.py:881
  104.9 16.4 %collective-permute-start.23 = (bf16[560,640]{1,0:T(8,128)(2,1)}, bf16[560,640]{1,0:T(8,128)(2,1)S(1)}, u32[]{:S(2)}, u32[]{:S(2)}) collective-permute-start(bf16[560,640]{1,0:T(8,128)(2,1)} %get-tuple-element.120), channel_id=1, source_target_pairs={{0,6},{1,3},{2,4},{3,1},{4,2},{5,7},{6,0},{7,5},{8,14},{9,11},{10,... | collective-permute-start | bytes 2150408 | tf_op jit(solution)/shard_map/ppermute | solution.py:881
  112.4 12.9 %collective-permute-start.11 = (bf16[576,640]{1,0:T(8,128)(2,1)S(1)}, bf16[576,640]{1,0:T(8,128)(2,1)S(1)}, u32[]{:S(2)}, u32[]{:S(2)}) collective-permute-start(bf16[576,640]{1,0:T(8,128)(2,1)S(1)} %get-tuple-element.85), channel_id=1, source_target_pairs={{0,96},{1,33},{2,98},{3,35},{4,100},{5,37},{6,102},{7,39},{8,104},... | collective-permute-start | bytes 2211848 | tf_op jit(solution)/shard_map/ppermute | solution.py:881
  115.6 11.8 %collective-permute-start.18 = (bf16[288,640]{1,0:T(8,128)(2,1)S(1)}, bf16[288,640]{1,0:T(8,128)(2,1)S(1)}, u32[]{:S(2)}, u32[]{:S(2)}) collective-permute-start(bf16[288,640]{1,0:T(8,128)(2,1)S(1)} %get-tuple-element.107), channel_id=1, source_target_pairs={{0,2},{1,7},{2,0},{3,5},{4,6},{5,3},{6,4},{7,1},{8,10},{9,15},{10,... | collective-permute-start | bytes 1105928 | tf_op jit(solution)/shard_map/ppermute | solution.py:881
  123.2 8.1 %collective-permute-start.24 = (bf16[288,640]{1,0:T(8,128)(2,1)S(1)}, bf16[288,640]{1,0:T(8,128)(2,1)S(1)}, u32[]{:S(2)}, u32[]{:S(2)}) collective-permute-start(bf16[288,640]{1,0:T(8,128)(2,1)S(1)} %get-tuple-element.122), channel_id=1, source_target_pairs={{0,32},{1,97},{2,34},{3,99},{4,36},{5,101},{6,38},{7,103},{8,40},{... | collective-permute-start | bytes 1105928 | tf_op jit(solution)/shard_map/ppermute | solution.py:881
  127.2 9.3 %collective-permute-start.12 = (bf16[304,640]{1,0:T(8,128)(2,1)S(1)}, bf16[304,640]{1,0:T(8,128)(2,1)S(1)}, u32[]{:S(2)}, u32[]{:S(2)}) collective-permute-start(bf16[304,640]{1,0:T(8,128)(2,1)S(1)} %get-tuple-element.88), channel_id=1, source_target_pairs={{0,8},{1,25},{2,10},{3,27},{4,12},{5,29},{6,14},{7,31},{8,0},{9,17... | collective-permute-start | bytes 1167368 | tf_op jit(solution)/shard_map/ppermute | solution.py:881
  129.5 15.4 %collective-permute-start.19 = (bf16[176,640]{1,0:T(8,128)(2,1)S(1)}, bf16[176,640]{1,0:T(8,128)(2,1)S(1)}, u32[]{:S(2)}, u32[]{:S(2)}) collective-permute-start(bf16[176,640]{1,0:T(8,128)(2,1)S(1)} %get-tuple-element.109), channel_id=1, source_target_pairs={{0,6},{1,3},{2,4},{3,1},{4,2},{5,7},{6,0},{7,5},{8,14},{9,11},{10,... | collective-permute-start | bytes 675848 | tf_op jit(solution)/shard_map/ppermute | solution.py:881
  133.5 11.7 %collective-permute-start.25 = (bf16[176,640]{1,0:T(8,128)(2,1)S(1)}, bf16[176,640]{1,0:T(8,128)(2,1)S(1)}, u32[]{:S(2)}, u32[]{:S(2)}) collective-permute-start(bf16[176,640]{1,0:T(8,128)(2,1)S(1)} %get-tuple-element.124), channel_id=1, source_target_pairs={{0,96},{1,33},{2,98},{3,35},{4,100},{5,37},{6,102},{7,39},{8,104},... | collective-permute-start | bytes 675848 | tf_op jit(solution)/shard_map/ppermute | solution.py:881
  138.7 11.8 %collective-permute-start.13 = (bf16[192,640]{1,0:T(8,128)(2,1)S(1)}, bf16[192,640]{1,0:T(8,128)(2,1)S(1)}, u32[]{:S(2)}, u32[]{:S(2)}) collective-permute-start(bf16[192,640]{1,0:T(8,128)(2,1)S(1)} %get-tuple-element.91), channel_id=1, source_target_pairs={{0,24},{1,9},{2,26},{3,11},{4,28},{5,13},{6,30},{7,15},{8,16},{9,1... | collective-permute-start | bytes 737288 | tf_op jit(solution)/shard_map/ppermute | solution.py:881
  145.3 5.4 %collective-permute-start.26 = (bf16[112,640]{1,0:T(8,128)(2,1)S(1)}, bf16[112,640]{1,0:T(8,128)(2,1)S(1)}, u32[]{:S(2)}, u32[]{:S(2)}) collective-permute-start(bf16[112,640]{1,0:T(8,128)(2,1)S(1)} %get-tuple-element.127), channel_id=1, source_target_pairs={{0,8},{1,25},{2,10},{3,27},{4,12},{5,29},{6,14},{7,31},{8,0},{9,17... | collective-permute-start | bytes 430088 | tf_op jit(solution)/shard_map/ppermute | solution.py:881
  150.3 5.7 %collective-permute-start.21 = (bf16[64,640]{1,0:T(8,128)(2,1)S(1)}, bf16[64,640]{1,0:T(8,128)(2,1)S(1)}, u32[]{:S(2)}, u32[]{:S(2)}) collective-permute-start(bf16[64,640]{1,0:T(8,128)(2,1)S(1)} %get-tuple-element.116), channel_id=1, source_target_pairs={{0,96},{1,33},{2,98},{3,35},{4,100},{5,37},{6,102},{7,39},{8,104},... | collective-permute-start | bytes 245768 | tf_op jit(solution)/shard_map/ppermute | solution.py:881
  150.6 6.0 %collective-permute-start.14 = (bf16[128,640]{1,0:T(8,128)(2,1)S(1)}, bf16[128,640]{1,0:T(8,128)(2,1)S(1)}, u32[]{:S(2)}, u32[]{:S(2)}) collective-permute-start(bf16[128,640]{1,0:T(8,128)(2,1)S(1)} %get-tuple-element.95), channel_id=1, source_target_pairs={{0,2},{1,7},{2,0},{3,5},{4,6},{5,3},{6,4},{7,1},{8,10},{9,15},{10,... | collective-permute-start | bytes 491528 | tf_op jit(solution)/shard_map/ppermute | solution.py:881
  150.8 5.7 %collective-permute-start.27 = (bf16[64,640]{1,0:T(8,128)(2,1)S(1)}, bf16[64,640]{1,0:T(8,128)(2,1)S(1)}, u32[]{:S(2)}, u32[]{:S(2)}) collective-permute-start(bf16[64,640]{1,0:T(8,128)(2,1)S(1)} %get-tuple-element.131), channel_id=1, source_target_pairs={{0,24},{1,9},{2,26},{3,11},{4,28},{5,13},{6,30},{7,15},{8,16},{9,1... | collective-permute-start | bytes 245768 | tf_op jit(solution)/shard_map/ppermute | solution.py:881
  156.7 8.2 %collective-permute-start.15 = (bf16[80,640]{1,0:T(8,128)(2,1)S(1)}, bf16[80,640]{1,0:T(8,128)(2,1)S(1)}, u32[]{:S(2)}, u32[]{:S(2)}) collective-permute-start(bf16[80,640]{1,0:T(8,128)(2,1)S(1)} %get-tuple-element.100), channel_id=1, source_target_pairs={{0,6},{1,3},{2,4},{3,1},{4,2},{5,7},{6,0},{7,5},{8,14},{9,11},{10,... | collective-permute-start | bytes 307208 | tf_op jit(solution)/shard_map/ppermute | solution.py:881
  (23 other events, 127.7 us)
